TPU v7x, 32 devices: a whole 2x2x4 slice. The times are simulated.
32 devices in a mesh: ch: 2 (over core), ty: 4 (over z), tx: 4 (over y, x).
Axes of the slice: x: 2, y: 2, z: 4, core: 2. Of those that a mesh axis runs over, the one named last changes fastest.
Arguments:
- image_plane: bfloat16 [4, 1024, 8192], P('ch', 'ty', 'tx'), may hold values from -12 to 12
- patch_shift: int32 [4, 2, 16, 128], P('ch', None, 'ty', 'tx'), may hold values from -36 to 36, as said below
Outputs:
- corrected: bfloat16 [4, 1024, 8192], P('ch', 'ty', 'tx')
Inputs may be any that keep to these rules, and one draw needn't show every extreme that they name: `patch_shift`: row components (index 0 of the second dimension) lie within -10 to 10 and reach both ends; column components reach both ends of the range.
All inputs are finite; a program needn't handle non-finite values.
Results may differ from a plain program's by a relative error of at most 0.034.
Values may be sent and summed in bfloat16 or wider, within the bound.
A program may use at most 64 MiB of HBM per device.

v0:
```python
import jax
import jax.numpy as jnp
from jax import lax
from jax.sharding import PartitionSpec as P

PATCH = 64
SPAN_Y = 256
SPAN_X = 512
MAX_Y = 12
MAX_X = 60
HALO_Y = 16
HALO_X = 64


EPS = 1e-05


def broadcast(block, axis, owner):
    block = jnp.where(lax.axis_index(axis) == owner, block, jnp.zeros_like(block))
    return lax.psum(block, axis)


def with_halo(array, sides, width):
    for axis, dim in sides:
        size, length = (lax.axis_size(axis), array.shape[dim])
        up = [(i, (i + 1) % size) for i in range(size - 1)]
        down = [(j, i) for i, j in up]
        last = lax.slice_in_dim(array, length - width, length, axis=dim)
        initial = lax.slice_in_dim(array, 0, width, axis=dim)
        before = lax.ppermute(last, axis, up)
        after = lax.ppermute(initial, axis, down)
        array = jnp.concatenate([before, array, after], axis=dim)
    return array


def bspline(offset):
    mag = jnp.abs(offset)
    near_part = 2.0 / 3.0 - mag * mag + 0.5 * mag * mag * mag
    far_part = (2.0 - mag) * (2.0 - mag) * (2.0 - mag) / 6.0
    return jnp.where(mag < 1.0, near_part, jnp.where(mag < 2.0, far_part, 0.0 * mag))


def cubic_kernel(offset):
    mag = jnp.abs(offset)
    near_part = (1.5 * mag - 2.5) * mag * mag + 1.0
    far_part = ((-0.5 * mag + 2.5) * mag - 4.0) * mag + 2.0
    return jnp.where(mag <= 1.0, near_part, jnp.where(mag < 2.0, far_part, 0.0 * mag))


def spline_basis(centers, control_count, spacing):
    knot_pos = jnp.arange(control_count, dtype=jnp.float32) - 1.0
    return bspline(centers[:, None] / spacing - knot_pos[None, :])


def penalty(control_count):
    identity = jnp.eye(control_count, dtype=jnp.float32)
    second_diff = identity[:-2] - 2.0 * identity[1:-1] + identity[2:]
    return jnp.dot(second_diff.T, second_diff, precision=lax.Precision.HIGHEST)


def patch_energy(planes):
    chan_count, row_count, col_count = planes.shape
    squared = planes.astype(jnp.float32) * planes.astype(jnp.float32)
    row_sums = squared.reshape(chan_count, row_count // PATCH, PATCH, col_count).sum(axis=2)
    block_sums = row_sums.reshape(chan_count, row_count // PATCH, col_count // PATCH, PATCH).sum(
        axis=3
    )
    return block_sums / (PATCH * PATCH) + EPS


def solve_spline(gram, rhs, smooth_weight, control_count):
    system = gram + smooth_weight * penalty(control_count)
    factor = jnp.linalg.cholesky(system)

    def solve_one(one_factor, one_rhs):
        return jax.scipy.linalg.cho_solve((one_factor, True), one_rhs)

    return jax.vmap(solve_one)(factor, rhs)


def local(image_plane, patch_shift):
    highest = lax.Precision.HIGHEST
    chan_count, row_count, col_count = image_plane.shape
    total_rows = row_count * lax.axis_size("ty")
    total_cols = col_count * lax.axis_size("tx")
    row_start = lax.axis_index("ty") * row_count
    col_start = lax.axis_index("tx") * col_count
    count_rows = total_rows // SPAN_Y + 3
    count_cols = total_cols // SPAN_X + 3
    own_energy = patch_energy(image_plane)
    ref_energy = broadcast(own_energy[0], "ch", 0)
    weight = jnp.sqrt(ref_energy[None] * own_energy)
    widened = with_halo(image_plane, (("tx", 2),), HALO_X)
    padded = with_halo(widened, (("ty", 1),), HALO_Y)
    shifts = patch_shift.astype(jnp.float32)
    patch_rows = (row_start + jnp.arange(row_count // PATCH, dtype=jnp.int32) * PATCH).astype(
        jnp.float32
    ) + PATCH / 2.0
    patch_cols = (col_start + jnp.arange(col_count // PATCH, dtype=jnp.int32) * PATCH).astype(
        jnp.float32
    ) + PATCH / 2.0
    row_basis = spline_basis(patch_rows, count_rows, SPAN_Y)
    col_basis = spline_basis(patch_cols, count_cols, SPAN_X)
    row_gram = jnp.einsum(
        "ik,ci,il->ckl", row_basis, weight.sum(axis=2), row_basis, precision=highest
    )
    row_rhs = jnp.einsum(
        "ik,ci->ck", row_basis, (weight * shifts[:, 0]).sum(axis=2), precision=highest
    )
    col_gram = jnp.einsum(
        "jk,cj,jl->ckl", col_basis, weight.sum(axis=1), col_basis, precision=highest
    )
    col_rhs = jnp.einsum(
        "jk,cj->ck", col_basis, (weight * shifts[:, 1]).sum(axis=1), precision=highest
    )
    row_gram, row_rhs, col_gram, col_rhs = lax.psum(
        (row_gram, row_rhs, col_gram, col_rhs), ("ty", "tx")
    )
    lam_rows = SPAN_Y / PATCH * (total_cols / PATCH) * (2.0 * row_count / SPAN_Y) ** 4
    lam_cols = SPAN_X / PATCH * (total_rows / PATCH) * (1.0 * col_count / SPAN_X) ** 4
    row_coef = solve_spline(row_gram, row_rhs, lam_rows, count_rows)
    col_coef = solve_spline(col_gram, col_rhs, lam_cols, count_cols)
    pixel_rows = (row_start + jnp.arange(row_count, dtype=jnp.int32)).astype(jnp.float32) + 0.5
    pixel_cols = (col_start + jnp.arange(col_count, dtype=jnp.int32)).astype(jnp.float32) + 0.5
    row_disp = MAX_Y * jnp.tanh(
        jnp.einsum(
            "yk,ck->cy", spline_basis(pixel_rows, count_rows, SPAN_Y), row_coef, precision=highest
        )
        / MAX_Y
    )
    col_disp = MAX_X * jnp.tanh(
        jnp.einsum(
            "xk,ck->cx", spline_basis(pixel_cols, count_cols, SPAN_X), col_coef, precision=highest
        )
        / MAX_X
    )
    source_rows = jnp.arange(row_count + 2 * HALO_Y, dtype=jnp.float32)
    target_rows = jnp.arange(row_count, dtype=jnp.float32)[None, :] + HALO_Y + row_disp
    row_taps = cubic_kernel(source_rows[None, :, None] - target_rows[:, None, :]).astype(
        jnp.bfloat16
    )
    rows_resampled = jnp.einsum(
        "cso,csx->cox", row_taps, padded, preferred_element_type=jnp.float32
    ).astype(jnp.bfloat16)
    block_cols = min(512, col_count)
    source_cols = jnp.arange(block_cols + 2 * HALO_X, dtype=jnp.float32)
    out_cols = jnp.arange(block_cols, dtype=jnp.float32)
    results = []
    for block_index in range(col_count // block_cols):
        start = block_index * block_cols
        window = rows_resampled[:, :, start : start + block_cols + 2 * HALO_X]
        target_cols = out_cols[None, :] + HALO_X + col_disp[:, start : start + block_cols]
        col_taps = cubic_kernel(source_cols[None, :, None] - target_cols[:, None, :]).astype(
            jnp.bfloat16
        )
        results.append(
            jnp.einsum("cos,csx->cox", window, col_taps, preferred_element_type=jnp.float32).astype(
                jnp.bfloat16
            )
        )
    return jnp.concatenate(results, axis=2)


def solution(mesh):
    return jax.shard_map(
        local,
        mesh=mesh,
        in_specs=(P("ch", "ty", "tx"), P("ch", None, "ty", "tx")),
        out_specs=P("ch", "ty", "tx"),
        check_vma=False,
    )
```

profile of v0, /device:TPU:0, one launch (start us, length us, event | category | flops | bytes accessed | tf_op | source)
XLA Modules:
  0.0 126.8 jit_solution(9848427046595813480)
XLA Ops:
  0.0 0.0 copy-start.1
  0.0 1.1 fusion.270
  1.1 1.3 %collective-permute-start.1 = (bf16[2,256,64]{2,1,0:T(8,128)(2,1)S(1)}, bf16[2,256,64]{2,1,0:T(8,128)(2,1)S(1)}, u32[]{:S(2)}, u32[]{:S(2)}) collective-permute-start(bf16[2,256,64]{2,1,0:T(8,128)(2,1)S(1)} %get-tuple-element.15), channel_id=1, source_target_pairs={{1,0},{2,1},{3,2},{5,4},{6,5},{7,6},{9,8},{10,9},{11,10},{13,12},{... | collective-permute-start | bytes 196616 | tf_op jit(solution)/shard_map/ppermute | solution.py:31
  2.4 5.5 %collective-permute-start = (bf16[2,256,64]{2,1,0:T(8,128)(2,1)S(1)}, bf16[2,256,64]{2,1,0:T(8,128)(2,1)S(1)}, u32[]{:S(2)}, u32[]{:S(2)}) collective-permute-start(bf16[2,256,64]{2,1,0:T(8,128)(2,1)S(1)} %get-tuple-element.16), channel_id=1, source_target_pairs={{0,1},{1,2},{2,3},{4,5},{5,6},{6,7},{8,9},{9,10},{10,11},{12,13},{... | collective-permute-start | bytes 196616 | tf_op jit(solution)/shard_map/ppermute | solution.py:30
  8.1 0.0 copy-start
  8.1 2.3 %bitcast_reduce_fusion = f32[2,4,2048]{2,1,0:T(4,128)S(1)} fusion(bf16[2,256,2048]{2,1,0:T(8,128)(2,1)} %param.2), kind=kLoop, calls=%fused_computation.1 | loop fusion | flops 3129344 | bytes 2162688 | tf_op jit(solution)/shard_map/reduce_sum | solution.py:64
  10.4 0.2 convolution_multiply_fusion.2
  10.6 0.1 copy.24
  10.7 0.0 copy-done.1
  10.7 0.2 convolution_multiply_fusion.1
  10.9 0.1 copy.31
  11.0 0.1 reshape.112
  11.1 0.1 reduce_sum.59
  11.3 2.5 %psum.35 = f32[4,32]{1,0:T(4,128)S(1)} all-reduce(f32[4,32]{1,0:T(4,128)S(1)} %fusion.198), channel_id=1, replica_groups=mesh['ch'=2,'ty'=4,'tx'=4] {'ch'}, use_global_device_ids=true, to_apply=%region_2.3 | all-reduce | flops 128 | bytes 1024 | tf_op jit(solution)/shard_map/psum | solution.py:20
  13.7 0.1 fusion.194
  13.8 0.1 fusion.168
  13.9 0.2 fusion.265
  14.1 0.1 fusion.139
  14.2 0.2 fusion.186
  14.4 0.2 fusion.169
  14.6 0.3 fusion.131
  14.9 75.5 %all-reduce = (f32[2,19]{1,0:T(2,128)S(1)}, f32[2,19,19]{1,2,0:T(8,128)S(1)}, f32[2,7,7]{1,2,0:T(8,128)S(1)}, f32[2,7]{1,0:T(2,128)S(1)}) all-reduce(f32[2,19]{1,0:T(2,128)S(1)} %fusion.186, f32[2,19,19]{1,2,0:T(8,128)S(1)} %fusion.131, f32[2,7,7]{1,2,0:T(8,128)S(1)} %fusion.169, ...), channel_id=1, replica_groups=mesh['ch'=2,'ty'=4,'tx'=4] {'ty','tx'}, use_global_device_ids=true, to_apply=%region_14.15 | all-reduce | flops 872 | bytes 6976 | tf_op jit(solution)/shard_map/psum | solution.py:116
  90.4 0.1 copy.25
  90.5 1.2 custom-call.22
  91.7 0.1 select_reduce_fusion.1
  91.8 0.1 compare_reduce_fusion.1
  91.9 0.1 select_bitcast_fusion.1
  92.0 1.1 custom-call.23
  93.1 0.1 copy.28
  93.2 0.1 copy.37
  93.3 0.1 convolution_bitcast_fusion.1
  93.5 0.1 fusion.271
  93.6 0.1 copy.32
  93.7 3.5 %custom-call.24 = f32[2,19,19]{2,1,0:T(8,128)S(1)} custom-call(f32[2,19,19]{2,1,0:T(8,128)S(1)} %fusion.130), custom_call_target="Cholesky" | custom-call | tf_op jit(solution)/shard_map/jit(cholesky)/cholesky | solution.py:73
  97.3 0.1 compare_reduce_fusion
  97.4 0.1 select_bitcast_fusion
  97.5 2.9 %custom-call.25 = f32[2,1,19,19]{2,3,1,0:T(8,128)S(1)} custom-call(f32[2,1,19,19]{3,2,1,0:T(8,128)S(1)} %select_bitcast_fusion), custom_call_target="InvertDiagBlocksLowerTriangular" | custom-call | tf_op jit(solution)/shard_map/vmap(jit(_cho_solve))/triangular_solve | solution.py:76
  100.4 0.2 convolution_bitcast_fusion
  100.6 0.2 fusion.127
  100.7 0.4 fusion.26
  101.2 0.0 collective-permute-done.1
  101.2 0.0 collective-permute-done
  101.2 0.0 copy-done
  101.2 3.7 %concatenate.9 = bf16[2,256,2176]{2,1,0:T(8,128)(2,1)} concatenate(bf16[2,256,64]{2,1,0:T(8,128)(2,1)S(1)} %collective-permute-done, bf16[2,256,2048]{2,1,0:T(8,128)(2,1)S(1)} %copy-done, bf16[2,256,64]{2,1,0:T(8,128)(2,1)S(1)} %collective-permute-done.1), dimensions={2} | concatenate | bytes 4456448 | tf_op jit(solution)/shard_map/concatenate | solution.py:32
  104.9 1.0 fusion.269
  105.9 1.3 %collective-permute-start.2 = (bf16[2,16,2176]{2,1,0:T(8,128)(2,1)S(1)}, bf16[2,16,2176]{2,1,0:T(8,128)(2,1)S(1)}, u32[]{:S(2)}, u32[]{:S(2)}) collective-permute-start(bf16[2,16,2176]{2,1,0:T(8,128)(2,1)S(1)} %get-tuple-element.13), channel_id=1, source_target_pairs={{0,4},{4,8},{8,12},{1,5},{5,9},{9,13},{2,6},{6,10},{10,14},{3,7},{... | collective-permute-start | bytes 417800 | tf_op jit(solution)/shard_map/ppermute | solution.py:30
  107.2 1.5 %collective-permute-start.3 = (bf16[2,16,2176]{2,1,0:T(8,128)(2,1)S(1)}, bf16[2,16,2176]{2,1,0:T(8,128)(2,1)S(1)}, u32[]{:S(2)}, u32[]{:S(2)}) collective-permute-start(bf16[2,16,2176]{2,1,0:T(8,128)(2,1)S(1)} %get-tuple-element.14), channel_id=1, source_target_pairs={{4,0},{8,4},{12,8},{5,1},{9,5},{13,9},{6,2},{10,6},{14,10},{7,3},{... | collective-permute-start | bytes 417800 | tf_op jit(solution)/shard_map/ppermute | solution.py:31
  108.7 0.2 fusion.85
  108.9 0.9 collective-permute-done.2
  109.8 4.4 %collective-permute-done.3 = bf16[2,16,2176]{2,1,0:T(8,128)(2,1)S(1)} collective-permute-done((bf16[2,16,2176]{2,1,0:T(8,128)(2,1)S(1)}, bf16[2,16,2176]{2,1,0:T(8,128)(2,1)S(1)}, u32[]{:S(2)}, u32[]{:S(2)}) %collective-permute-start.3) | collective-permute-done | bytes 139296 | tf_op jit(solution)/shard_map/ppermute | solution.py:31
  114.2 3.2 %convolution_convert_fusion = bf16[2,256,2176]{2,1,0:T(8,128)(2,1)S(1)} fusion(bf16[2,16,2176]{2,1,0:T(8,128)(2,1)S(1)} %collective-permute-done.3, bf16[2,256,2176]{2,1,0:T(8,128)(2,1)} %concatenate.9, bf16[2,16,2176]{2,1,0:T(8,128)(2,1)S(1)} %collective-permute-done.2, f32[2,256]{1,0:T(2,128)S(1)} %fusion.85), kind=kOutput, calls=%fused_computation | convolution fusion | flops 653164544 | bytes 4737024 | tf_op jit(solution)/shard_map/cso,csx->cox/dot_general | solution.py:142
  117.4 1.9 %fusion.80 = bf16[2,256,512]{2,1,0:T(8,128)(2,1)S(1)} fusion(f32[2,512]{1,0:T(2,128)S(1)} %get-tuple-element.18, bf16[2,256,2176]{2,1,0:T(8,128)(2,1)S(1)} %convolution_convert_fusion), kind=kOutput, calls=%fused_computation.83 | convolution fusion | flops 348258304 | bytes 1183744 | tf_op jit(solution)/shard_map/cos,csx->cox/dot_general | solution.py:157
  119.3 1.9 %fusion.77 = bf16[2,256,512]{2,1,0:T(8,128)(2,1)S(1)} fusion(f32[2,512]{1,0:T(2,128)S(1)} %get-tuple-element.19, bf16[2,256,2176]{2,1,0:T(8,128)(2,1)S(1)} %convolution_convert_fusion), kind=kOutput, calls=%fused_computation.82 | convolution fusion | flops 348258304 | bytes 1183744 | tf_op jit(solution)/shard_map/cos,csx->cox/dot_general | solution.py:157
  121.2 1.9 %fusion.74 = bf16[2,256,512]{2,1,0:T(8,128)(2,1)S(1)} fusion(f32[2,512]{1,0:T(2,128)S(1)} %get-tuple-element.20, bf16[2,256,2176]{2,1,0:T(8,128)(2,1)S(1)} %convolution_convert_fusion), kind=kOutput, calls=%fused_computation.81 | convolution fusion | flops 348258304 | bytes 1183744 | tf_op jit(solution)/shard_map/cos,csx->cox/dot_general | solution.py:157
  123.2 1.9 %fusion.71 = bf16[2,256,512]{2,1,0:T(8,128)(2,1)S(1)} fusion(f32[2,512]{1,0:T(2,128)S(1)} %get-tuple-element.17, bf16[2,256,2176]{2,1,0:T(8,128)(2,1)S(1)} %convolution_convert_fusion), kind=kOutput, calls=%fused_computation.80 | convolution fusion | flops 348258304 | bytes 1183744 | tf_op jit(solution)/shard_map/cos,csx->cox/dot_general | solution.py:157
  125.1 1.6 %pad_maximum_fusion = bf16[2,256,2048]{2,1,0:T(8,128)(2,1)} fusion(bf16[2,256,512]{2,1,0:T(8,128)(2,1)S(1)} %fusion.80, bf16[2,256,512]{2,1,0:T(8,128)(2,1)S(1)} %fusion.77, bf16[2,256,512]{2,1,0:T(8,128)(2,1)S(1)} %fusion.74, bf16[2,256,512]{2,1,0:T(8,128)(2,1)S(1)} %fusion.71), kind=kLoop, calls=%fused_computation.39 | loop fusion | flops 8388608 | bytes 4194304 | tf_op jit(solution)/shard_map/concatenate | solution.py:161
  (23 shorter events, 0.2 us)
Async XLA Ops:
  0.0 10.7 %copy-start.1 = (s32[2,2,4,32]{3,2,1,0:T(4,128)S(1)}, s32[2,2,4,32]{3,2,1,0:T(4,128)}, u32[]{:S(2)}) copy-start(s32[2,2,4,32]{3,2,1,0:T(4,128)} %param.3) | copy-start | bytes 6148
  1.1 100.1 %collective-permute-start.1 = (bf16[2,256,64]{2,1,0:T(8,128)(2,1)S(1)}, bf16[2,256,64]{2,1,0:T(8,128)(2,1)S(1)}, u32[]{:S(2)}, u32[]{:S(2)}) collective-permute-start(bf16[2,256,64]{2,1,0:T(8,128)(2,1)S(1)} %get-tuple-element.15), channel_id=1, source_target_pairs={{1,0},{2,1},{3,2},{5,4},{6,5},{7,6},{9,8},{10,9},{11,10},{13,12},{... | collective-permute-start | bytes 196616 | tf_op jit(solution)/shard_map/ppermute | solution.py:31
  2.4 98.8 %collective-permute-start = (bf16[2,256,64]{2,1,0:T(8,128)(2,1)S(1)}, bf16[2,256,64]{2,1,0:T(8,128)(2,1)S(1)}, u32[]{:S(2)}, u32[]{:S(2)}) collective-permute-start(bf16[2,256,64]{2,1,0:T(8,128)(2,1)S(1)} %get-tuple-element.16), channel_id=1, source_target_pairs={{0,1},{1,2},{2,3},{4,5},{5,6},{6,7},{8,9},{9,10},{10,11},{12,13},{... | collective-permute-start | bytes 196616 | tf_op jit(solution)/shard_map/ppermute | solution.py:30
  8.1 93.1 %copy-start = (bf16[2,256,2048]{2,1,0:T(8,128)(2,1)S(1)}, bf16[2,256,2048]{2,1,0:T(8,128)(2,1)}, u32[]{:S(2)}) copy-start(bf16[2,256,2048]{2,1,0:T(8,128)(2,1)} %param.2) | copy-start | bytes 6291460
  105.9 3.9 %collective-permute-start.2 = (bf16[2,16,2176]{2,1,0:T(8,128)(2,1)S(1)}, bf16[2,16,2176]{2,1,0:T(8,128)(2,1)S(1)}, u32[]{:S(2)}, u32[]{:S(2)}) collective-permute-start(bf16[2,16,2176]{2,1,0:T(8,128)(2,1)S(1)} %get-tuple-element.13), channel_id=1, source_target_pairs={{0,4},{4,8},{8,12},{1,5},{5,9},{9,13},{2,6},{6,10},{10,14},{3,7},{... | collective-permute-start | bytes 417800 | tf_op jit(solution)/shard_map/ppermute | solution.py:30
  107.2 6.9 %collective-permute-start.3 = (bf16[2,16,2176]{2,1,0:T(8,128)(2,1)S(1)}, bf16[2,16,2176]{2,1,0:T(8,128)(2,1)S(1)}, u32[]{:S(2)}, u32[]{:S(2)}) collective-permute-start(bf16[2,16,2176]{2,1,0:T(8,128)(2,1)S(1)} %get-tuple-element.14), channel_id=1, source_target_pairs={{4,0},{8,4},{12,8},{5,1},{9,5},{13,9},{6,2},{10,6},{14,10},{7,3},{... | collective-permute-start | bytes 417800 | tf_op jit(solution)/shard_map/ppermute | solution.py:31
where the time goes:
time: 127 us
  blocking collectives  78 us (61%)
  other arithmetic  13.7 us (11%)
  matrix products  13.5 us (11%)
  starting transfers between devices  9.54 us (8%)
  local copies, waits for them, and re-layouts  6.55 us (5%)
  waiting for transfers between devices  5.26 us (4%)
    psum x1, blocking collectives, local(): lax.psum((row_gram, row_rhs, col_gram, col_rhs), ('ty', 'tx'))  75.5 us
    dot_general x4, matrix products, local(): jnp.einsum('cos,csx->cox', window, col_taps, preferred_element_type=jnp.f...  7.75 us
    ppermute x2, starting transfers between devices, with_halo(): before = lax.ppermute(last, axis, up)  6.78 us
    another operation x8, other arithmetic, solve_spline(): factor = jnp.linalg.cholesky(system)  5.08 us
    ppermute x2, waiting for transfers between devices, with_halo(): after = lax.ppermute(initial, axis, down)  4.38 us
    another operation x6, other arithmetic, solve_one(): return jax.scipy.linalg.cho_solve((one_factor, True), one_rhs)  4.18 us
    concatenate x1, local copies, waits for them, and re-layouts, with_halo(): array = jnp.concatenate([before, array, after], axis=dim)  3.72 us
    dot_general x1, matrix products, local(): jnp.einsum('cso,csx->cox', row_taps, padded, preferred_element_type=jnp.f...  3.18 us
  transfers between devices with their start and end apart: 4, of which 2 were waited for; matrix products, arithmetic and copies ran while one was open for 12% of the time, Pallas kernels for 0%

commit v1 on v0

v1 whole, which is shorter than its diff:
```python
import functools

import jax
import jax.numpy as jnp
from jax import lax
from jax.experimental import pallas as pl
from jax.experimental.pallas import tpu as pltpu
from jax.sharding import PartitionSpec as P

PATCH = 64
SPAN_Y = 256
SPAN_X = 512
MAX_Y = 12
MAX_X = 60
HY = 16
HX = 128
EPS = 1e-05
LANES = 128
MESH = pl.DeviceIdType.MESH


def bspline(offset):
    mag = jnp.abs(offset)
    near_part = 2.0 / 3.0 - mag * mag + 0.5 * mag * mag * mag
    far_part = (2.0 - mag) * (2.0 - mag) * (2.0 - mag) / 6.0
    return jnp.where(mag < 1.0, near_part, jnp.where(mag < 2.0, far_part, 0.0))


def cubic_kernel(offset):
    a = jnp.maximum(2.0 - jnp.abs(offset), 0.0)
    c = a - 1.0
    b = jnp.maximum(c, 0.0)
    return a * a * (0.5 * c) + b * b * (1.0 - 2.0 * b)


def penalty_band(count):
    band = [[0.0] * count for _ in range(4)]
    coef = (1.0, -2.0, 1.0)
    for q in range(count - 2):
        for a in range(3):
            for b in range(a, 3):
                band[b - a][q + a] += coef[a] * coef[b]
    return band


def iota(dim, shape=(8, LANES)):
    return lax.broadcasted_iota(jnp.int32, shape, dim)


def repeat_for(start, stop, body):
    if stop - start <= 16:
        for i in range(start, stop):
            body(i)
    else:
        lax.fori_loop(start, stop, lambda i, _: (body(i), 0)[1], 0)


def fit_kernel(n_ty, n_tx, lam_y, lam_x, img_hbm, shift_ref, pad_hbm, col_ref, row_ref,
               img_v, sums_v, shift_v, e0_v, msg_v, slots_v, coef_v, zero_r, zero_c,
               img_sem, own_sem, zero_sem, e0_send, e0_recv, msg_send, msg_recv,
               halo_send, halo_recv):
    chans, rows, cols = img_v.shape
    prow, pcol = rows // PATCH, cols // PATCH
    n = n_ty * n_tx
    ch, ty, tx = lax.axis_index("ch"), lax.axis_index("ty"), lax.axis_index("tx")
    me = ty * n_tx + tx

    def peer_id(p):
        peer = lax.rem(me + p, n)
        return peer, {"ty": peer // n_tx, "tx": lax.rem(peer, n_tx)}

    barrier = pltpu.get_barrier_semaphore()
    partner = {"ch": 1 - ch}
    pl.semaphore_signal(barrier, inc=1, device_id=partner, device_id_type=MESH)

    def greet(p):
        _, where = peer_id(p)
        pl.semaphore_signal(barrier, inc=1, device_id=where, device_id_type=MESH)

    loads = []
    for c in range(chans):
        for i in range(prow):
            copy = pltpu.make_async_copy(
                img_hbm.at[c, pl.ds(i * PATCH, PATCH)],
                img_v.at[c, pl.ds(i * PATCH, PATCH)],
                img_sem.at[c * prow + i],
            )
            copy.start()
            loads.append(copy)
    repeat_for(1, n, greet)
    zero_r[...] = jnp.zeros_like(zero_r)
    zero_c[...] = jnp.zeros_like(zero_c)

    sub, lane = iota(0), iota(1)
    per_chan = 2 * prow
    per_dev = chans * per_chan
    ty_block = LANES // per_dev
    blocks = (n_ty + ty_block - 1) // ty_block
    col_sys = sub < chans
    row_sys = (sub >= chans) & (sub < 2 * chans)
    is_rhs = jnp.where(col_sys, (lane // pcol) % 2, (lane // prow) % 2) == 1
    key_y = n_ty * rows // SPAN_Y + 3
    key_x = n_tx * cols // SPAN_X + 3
    per_y, per_x = rows * ty_block // SPAN_Y, cols // SPAN_X
    keys = max(key_y, key_x)
    chunks = max(n_tx, blocks)
    col_pos = (lane % pcol * PATCH).astype(jnp.float32) / SPAN_X + (PATCH / 2.0 / SPAN_X + 1.0)
    row_index = lane // per_dev * prow + lane % prow
    row_pos = (row_index * PATCH).astype(jnp.float32) / SPAN_Y + (PATCH / 2.0 / SPAN_Y + 1.0)
    for q in range(2):
        for c in range(chans):
            part = shift_ref[c, q].astype(jnp.float32)
            for g in range(LANES // pcol):
                shift_v[q, pl.ds(c * prow, prow), pl.ds(g * pcol, pcol)] = part
    ind = (iota(0, (LANES, LANES)) // PATCH == iota(1, (LANES, LANES)) % 2).astype(jnp.float32)

    for c in range(chans):
        for i in range(prow):
            loads[c * prow + i].wait()
            for t in range(cols // LANES):
                part = img_v[c, pl.ds(i * PATCH, PATCH), pl.ds(t * LANES, LANES)].astype(jnp.float32)
                sums_v[pl.ds(t * 8 + c * prow + i, 1), :] = jnp.sum(part * part, axis=0, keepdims=True)
    owns = [
        pltpu.make_async_copy(
            img_v.at[c], pad_hbm.at[c, pl.ds(HY, rows), pl.ds(HX, cols)], own_sem.at[c]
        )
        for c in range(chans)
    ]
    halves = jnp.dot(sums_v[...], ind, precision=lax.Precision.HIGHEST,
                     preferred_element_type=jnp.float32)
    energy = jnp.zeros((8, LANES), jnp.float32)
    for t in range(cols // LANES):
        energy = jnp.where(lane % pcol // 2 == t, halves[t * 8 : t * 8 + 8], energy)
    energy = energy / (PATCH * PATCH) + EPS

    pl.semaphore_wait(barrier, n)
    e0_copy = pltpu.make_async_remote_copy(
        src_ref=e0_v, dst_ref=e0_v, send_sem=e0_send, recv_sem=e0_recv,
        device_id=partner, device_id_type=MESH,
    )

    @pl.when(ch == 0)
    def _():
        e0_v[...] = energy
        e0_copy.start()

    @pl.when(ch == 1)
    def _():
        e0_copy.wait_recv()

    ref_energy = jnp.concatenate([e0_v[0:prow]] * chans, axis=0)
    weight = jnp.sqrt(ref_energy * energy)
    mine = sub // prow == lane // (2 * pcol)
    scaled = jnp.where((lane // pcol) % 2 == 1, weight * shift_v[1], weight)
    msg_v[0:1, :] = jnp.sum(jnp.where(mine, scaled, 0.0), axis=0, keepdims=True)
    first = lane < pcol
    w_rows = jnp.sum(jnp.where(first, weight, 0.0), axis=1, keepdims=True)
    ws_rows = jnp.sum(jnp.where(first, weight * shift_v[0], 0.0), axis=1, keepdims=True)
    base = lax.rem(ty, ty_block) * per_dev + sub // prow * per_chan + sub % prow
    spread = jnp.where(lane == base, w_rows, jnp.where(lane == base + prow, ws_rows, 0.0))
    msg_v[1:2, :] = jnp.sum(spread, axis=0, keepdims=True)
    slots_v[me, 0:2] = msg_v[0:2]

    def msg_copy(p, slot):
        _, where = peer_id(p)
        return pltpu.make_async_remote_copy(
            src_ref=msg_v.at[pl.ds(0, 2)], dst_ref=slots_v.at[slot, pl.ds(0, 2)],
            send_sem=msg_send.at[p], recv_sem=msg_recv.at[slot],
            device_id=where, device_id_type=MESH,
        )

    repeat_for(1, n, lambda p: msg_copy(p, me).start())

    span_y = {1: (rows - HY, 0, HY), -1: (0, HY + rows, HY), 0: (0, HY, rows)}
    span_x = {1: (cols - HX, 0, HX), -1: (0, HX + cols, HX), 0: (0, HX, cols)}
    sides = [(0, 1), (0, -1), (1, 0), (-1, 0), (1, 1), (1, -1), (-1, 1), (-1, -1)]
    halos, fills = [], []
    for s, (dy, dx) in enumerate(sides):
        sy, qy, ly = span_y[dy]
        sx, qx, lx = span_x[dx]
        dst = pad_hbm.at[:, pl.ds(qy, ly), pl.ds(qx, lx)]
        to_y, to_x = ty + dy, tx + dx
        from_y, from_x = ty - dy, tx - dx
        has_to = (to_y >= 0) & (to_y < n_ty) & (to_x >= 0) & (to_x < n_tx)
        has_from = (from_y >= 0) & (from_y < n_ty) & (from_x >= 0) & (from_x < n_tx)
        halo = pltpu.make_async_remote_copy(
            src_ref=img_v.at[:, pl.ds(sy, ly), pl.ds(sx, lx)], dst_ref=dst,
            send_sem=halo_send.at[s], recv_sem=halo_recv.at[s],
            device_id={"ty": to_y, "tx": to_x}, device_id_type=MESH,
        )
        zeros = zero_c if ly == rows else zero_r
        fill = pltpu.make_async_copy(
            zeros.at[:, pl.ds(0, ly), pl.ds(0, lx)], dst, zero_sem.at[s]
        )
        pl.when(has_to)(halo.start)
        pl.when(jnp.logical_not(has_from))(fill.start)
        halos.append((halo, has_to, has_from, fill))
    for own in owns:
        own.start()

    bases = {}
    for t in range(chunks):
        span = set()
        if t < n_tx:
            span |= set(range(t * per_x, t * per_x + per_x + 3))
        if t < blocks:
            span |= set(range(t * per_y, t * per_y + per_y + 3))
        for k in sorted(span):
            if k < keys:
                local = jnp.where(col_sys, col_pos + (t * per_x - k), row_pos + (t * per_y - k))
                bases[k, t] = bspline(local.astype(jnp.float32))

    def msg_wait(p):
        peer, _ = peer_id(p)
        msg_copy(p, peer).wait_recv()

    repeat_for(1, n, msg_wait)

    data_w, data_r = [], []
    for t in range(chunks):
        data = jnp.zeros((8, LANES), jnp.float32)
        if t < n_tx:
            total = slots_v[t, 0:1]
            for y in range(1, n_ty):
                total = total + slots_v[y * n_tx + t, 0:1]
            data = jnp.where(col_sys & (lane // (2 * pcol) == sub), total, data)
        if t < blocks:
            low, high = t * ty_block * n_tx, min(n_ty, (t + 1) * ty_block) * n_tx
            total = slots_v[low, 1:2]
            for y in range(low + 1, high):
                total = total + slots_v[y, 1:2]
            data = jnp.where(row_sys & (lane % per_dev // per_chan == sub - chans), total, data)
        data_w.append(jnp.where(is_rhs, 0.0, data))
        data_r.append(jnp.where(is_rhs, data, 0.0))

    pen_y, pen_x = penalty_band(key_y), penalty_band(key_x)

    def added(d, k):
        rest = 1.0 if d == 0 else 0.0
        at_x = lam_x * pen_x[d][k] if k < key_x else rest
        at_y = lam_y * pen_y[d][k] if k < key_y else rest
        if at_x == at_y == rest:
            return rest
        return jnp.where(col_sys, at_x, jnp.where(row_sys, at_y, rest))

    band, rhs = {}, []
    for k in range(keys):
        for d in range(4):
            if k + d >= keys:
                continue
            total = None
            for t in range(chunks):
                if (k, t) in bases and (k + d, t) in bases:
                    term = bases[k, t] * bases[k + d, t] * data_w[t]
                    total = term if total is None else total + term
            if total is None:
                band[k, d] = jnp.zeros((8, LANES), jnp.float32) + added(d, k)
            else:
                band[k, d] = jnp.broadcast_to(jnp.sum(total, axis=1, keepdims=True), (8, LANES)) + added(d, k)
        total = None
        for t in range(chunks):
            if (k, t) in bases:
                term = bases[k, t] * data_r[t]
                total = term if total is None else total + term
        rhs.append(jnp.broadcast_to(jnp.sum(total, axis=1, keepdims=True), (8, LANES)))

    recips = []
    for k in range(keys):
        recip = 1.0 / band[k, 0]
        recips.append(recip)
        for e in range(1, 4):
            if k + e >= keys:
                break
            factor = band[k, e] * recip
            for f in range(e, 4):
                if k + f < keys:
                    band[k + e, f - e] = band[k + e, f - e] - factor * band[k, f]
            rhs[k + e] = rhs[k + e] - factor * rhs[k]
    solved = [None] * keys
    for k in reversed(range(keys)):
        value = rhs[k]
        for e in range(3, 0, -1):
            if k + e < keys:
                value = value - band[k, e] * solved[k + e]
        solved[k] = value * recips[k]
        coef_v[k] = solved[k]

    lane_f = lane.astype(jnp.float32) + 0.5
    for out_ref, span, size, start, bound in (
        (col_ref, SPAN_X, cols, tx * (cols // SPAN_X), MAX_X),
        (row_ref, SPAN_Y, rows, ty * (rows // SPAN_Y), MAX_Y),
    ):
        tiles = span // LANES
        shape = [
            [bspline((lane_f + u * LANES) / span - e + 1.0) for e in range(4)] for u in range(tiles)
        ]
        for q in range(size // span):
            coefs = [coef_v[start + q + e] for e in range(4)]
            for u in range(tiles):
                total = coefs[0] * shape[u][0]
                for e in range(1, 4):
                    total = total + coefs[e] * shape[u][e]
                at = (q * tiles + u) * LANES
                out_ref[:, at : at + LANES] = bound * jnp.tanh(total / bound)

    for halo, has_to, has_from, fill in halos:
        pl.when(has_from)(halo.wait_recv)
        pl.when(jnp.logical_not(has_from))(fill.wait)
        pl.when(has_to)(halo.wait_send)
    for own in owns:
        own.wait()
    pl.when(ch == 0)(e0_copy.wait_send)
    repeat_for(1, n, lambda p: msg_copy(p, me).wait_send())


BLOCK = 256
HALF = 128


def warp_kernel(pad_ref, col_ref, row_ref, out_ref, rows_v, rtaps_v, ctaps_v):
    c, b = pl.program_id(0), pl.program_id(1)
    rows = out_ref.shape[1]
    depth = pad_ref.shape[1]

    @pl.when((c == 0) & (b == 0))
    def _():
        ctaps_v[...] = jnp.zeros_like(ctaps_v)

    @pl.when(b == 0)
    def _():
        rows_v[...] = jnp.zeros_like(rows_v)
        disp = jnp.where(c == 0, row_ref[2:3, :], row_ref[3:4, :])
        target = lax.broadcasted_iota(jnp.int32, (1, rows), 1).astype(jnp.float32) + HY + disp
        source = lax.broadcasted_iota(jnp.int32, (depth, rows), 0).astype(jnp.float32)
        rtaps_v[...] = cubic_kernel(source - target).T.astype(jnp.bfloat16)

    rows_v[:, 0:BLOCK] = rows_v[:, BLOCK : 2 * BLOCK]
    rows_v[:, BLOCK : 2 * BLOCK] = jnp.dot(
        rtaps_v[...], pad_ref[0], preferred_element_type=jnp.float32
    ).astype(jnp.bfloat16)
    first = jnp.maximum(b - 1, 0) * BLOCK
    source = lax.broadcasted_iota(jnp.int32, (2 * HALF, HALF), 0).astype(jnp.float32)
    for h in range(BLOCK // HALF):
        at = pl.ds(pl.multiple_of(first + h * HALF, HALF), HALF)
        disp = jnp.where(c == 0, col_ref[0:1, at], col_ref[1:2, at])
        target = lax.broadcasted_iota(jnp.int32, (1, HALF), 1).astype(jnp.float32) + 64.0 + disp
        ctaps_v[64 + h * HALF : 64 + h * HALF + 2 * HALF, h * HALF : (h + 1) * HALF] = cubic_kernel(
            source - target
        ).astype(jnp.bfloat16)
    out_ref[0] = jnp.dot(
        rows_v[...], ctaps_v[...], preferred_element_type=jnp.float32
    ).astype(jnp.bfloat16)


def local(image_plane, patch_shift):
    n_ty, n_tx = lax.axis_size("ty"), lax.axis_size("tx")
    chans, rows, cols = image_plane.shape
    n = n_ty * n_tx
    lam_y = SPAN_Y / PATCH * (cols * n_tx / PATCH) * (2.0 * rows / SPAN_Y) ** 4
    lam_x = SPAN_X / PATCH * (rows * n_ty / PATCH) * (1.0 * cols / SPAN_X) ** 4
    keys = max(n_ty * rows // SPAN_Y, n_tx * cols // SPAN_X) + 3
    high, wide = rows + 2 * HY, cols + 2 * HX
    f32 = jnp.float32
    dma = pltpu.SemaphoreType.DMA
    vmem = pl.BlockSpec(memory_space=pltpu.VMEM)
    hbm = pl.BlockSpec(memory_space=pl.ANY)
    padded, col_disp, row_disp = pl.pallas_call(
        functools.partial(fit_kernel, n_ty, n_tx, lam_y, lam_x),
        out_shape=(
            jax.ShapeDtypeStruct((chans, high, wide), jnp.bfloat16),
            jax.ShapeDtypeStruct((8, cols), f32),
            jax.ShapeDtypeStruct((8, rows), f32),
        ),
        in_specs=[hbm, vmem],
        out_specs=(hbm, vmem, vmem),
        scratch_shapes=[
            pltpu.VMEM((chans, rows, cols), jnp.bfloat16),
            pltpu.VMEM((LANES, LANES), f32),
            pltpu.VMEM((2, 8, LANES), f32),
            pltpu.VMEM((8, LANES), f32),
            pltpu.VMEM((8, LANES), f32),
            pltpu.VMEM((n, 8, LANES), f32),
            pltpu.VMEM((keys, 8, LANES), f32),
            pltpu.VMEM((chans, HY, cols), jnp.bfloat16),
            pltpu.VMEM((chans, rows, HX), jnp.bfloat16),
            dma((8,)), dma((chans,)), dma((8,)), dma, dma,
            dma((n,)), dma((n,)), dma((8,)), dma((8,)),
        ],
        compiler_params=pltpu.CompilerParams(
            collective_id=0, has_side_effects=True, vmem_limit_bytes=32 * 2**20
        ),
    )(image_plane, patch_shift)
    steps = cols // BLOCK
    return pl.pallas_call(
        warp_kernel,
        grid=(chans, steps + 1),
        out_shape=jax.ShapeDtypeStruct((chans, rows, cols), jnp.bfloat16),
        in_specs=[
            pl.BlockSpec((1, high, BLOCK), lambda c, b: (c, 0, b)),
            pl.BlockSpec((8, cols), lambda c, b: (0, 0)),
            pl.BlockSpec((8, rows), lambda c, b: (0, 0)),
        ],
        out_specs=pl.BlockSpec((1, rows, BLOCK), lambda c, b: (c, 0, jnp.maximum(b - 1, 0))),
        scratch_shapes=[
            pltpu.VMEM((rows, 2 * BLOCK), jnp.bfloat16),
            pltpu.VMEM((rows, high), jnp.bfloat16),
            pltpu.VMEM((2 * BLOCK, BLOCK), jnp.bfloat16),
        ],
        compiler_params=pltpu.CompilerParams(vmem_limit_bytes=32 * 2**20),
    )(padded, col_disp, row_disp)


def solution(mesh):
    return jax.shard_map(
        local,
        mesh=mesh,
        in_specs=(P("ch", "ty", "tx"), P("ch", None, "ty", "tx")),
        out_specs=P("ch", "ty", "tx"),
        check_vma=False,
    )
```

time: 127 us -> 29.1 us (0.23)
  blocking collectives: 78 us -> 0 us
  Pallas kernels: 0 us -> 26.6 us
  other arithmetic: 13.7 us -> 0 us
  matrix products: 13.5 us -> 0 us
  starting transfers between devices: 9.54 us -> 0 us
  waiting for transfers between devices: 5.26 us -> 0 us
  local copies, waits for them, and re-layouts: 6.55 us -> 2.29 us
    psum x2 -> x0, blocking collectives: 78 us -> none  [the longest x1 75.5 us: local(): lax.psum((row_gram, row_rhs, col_gram, col_rhs), ('ty', 'tx'))]
    pallas_call x0 -> x2, Pallas kernels: none -> 26.6 us  [the longest x1 15.8 us: local(): pl.pallas_call(functools.partial(fit_kernel, n_ty, n_tx, lam_y, lam_x), o...]
    dot_general x13 -> x0, matrix products: 12.8 us -> none  [the longest x4 7.75 us: local(): jnp.einsum('cos,csx->cox', window, col_taps, preferred_element_type=jnp.f...]
    ppermute x4 -> x0, starting transfers between devices: 9.54 us -> none  [the longest x2 6.78 us: with_halo(): before = lax.ppermute(last, axis, up)]
    another operation x14 -> x0, other arithmetic: 9.26 us -> none  [the longest x8 5.08 us: solve_spline(): factor = jnp.linalg.cholesky(system)]
    ppermute x4 -> x0, waiting for transfers between devices: 5.26 us -> none  [the longest x2 4.38 us: with_halo(): after = lax.ppermute(initial, axis, down)]
    concatenate x1 -> x0, local copies, waits for them, and re-layouts: 3.72 us -> none  [with_halo(): array = jnp.concatenate([before, array, after], axis=dim)]
    reduce_sum x3 -> x0, other arithmetic: 2.48 us -> none  [the longest x1 2.27 us: patch_energy(): squared.reshape(chan_count, row_count // PATCH, PATCH, col_count)]
  transfers between devices with their start and end apart: 4 -> 0, of which waited for: 2 -> 0; matrix products, arithmetic and copies ran while one was open for 12% -> 0% of each run, Pallas kernels for 0% -> 0%
where the time goes in v1:
time: 29.1 us; the launch traced here: 28.9 us
  Pallas kernels  26.6 us (91%)
  local copies, waits for them, and re-layouts  2.29 us (8%)
    pallas_call x1, Pallas kernels, local(): pl.pallas_call(functools.partial(fit_kernel, n_ty, n_tx, lam_y, lam_x), o...  15.8 us
    pallas_call x1, Pallas kernels, local(): pl.pallas_call(warp_kernel, grid=(chans, steps + 1), out_shape=jax.ShapeD...  10.8 us
    unnamed x4, local copies, waits for them, and re-layouts  2.29 us

profile of v1, /device:TPU:0, one launch (start us, length us, event | category | flops | bytes accessed | tf_op | source)
XLA Modules:
  0.0 28.9 jit_solution(8846892676240969636)
XLA Ops:
  0.0 0.0 copy-start
  0.0 1.6 %copy-done = bf16[2,256,2048]{2,1,0:T(8,128)(2,1)S(1)} copy-done((bf16[2,256,2048]{2,1,0:T(8,128)(2,1)S(1)}, bf16[2,256,2048]{2,1,0:T(8,128)(2,1)}, u32[]{:S(2)}) %copy-start) | copy-done | bytes 2097176
  1.6 0.0 copy-start.1
  1.6 0.7 %copy-done.1 = s32[2,2,4,32]{3,2,1,0:T(4,128)S(1)} copy-done((s32[2,2,4,32]{3,2,1,0:T(4,128)S(1)}, s32[2,2,4,32]{3,2,1,0:T(4,128)}, u32[]{:S(2)}) %copy-start.1) | copy-done | bytes 2072
  2.3 15.8 %shard_map.28 = (bf16[2,288,2304]{2,1,0:T(8,128)(2,1)S(1)}, f32[8,2048]{1,0:T(8,128)S(1)}, f32[8,256]{1,0:T(8,128)S(1)}) custom-call(bf16[2,256,2048]{2,1,0:T(8,128)(2,1)S(1)} %copy-done, s32[2,2,4,32]{3,2,1,0:T(4,128)S(1)} %copy-done.1), custom_call_target="tpu_custom_call" | custom-call | tf_op jit(solution)/shard_map/pallas_call | solution.py:367
  18.1 10.8 %shard_map.29 = bf16[2,256,2048]{2,1,0:T(8,128)(2,1)} custom-call(bf16[2,288,2304]{2,1,0:T(8,128)(2,1)S(1)} %get-tuple-element.8.pad_ref, f32[8,2048]{1,0:T(8,128)S(1)} %get-tuple-element.9.col_ref, f32[8,256]{1,0:T(8,128)S(1)} %get-tuple-element.10.row_ref), custom_call_target="tpu_custom_call" | custom-call | tf_op jit(solution)/shard_map/pallas_call | solution.py:394
Async XLA Ops:
  0.0 1.6 %copy-start = (bf16[2,256,2048]{2,1,0:T(8,128)(2,1)S(1)}, bf16[2,256,2048]{2,1,0:T(8,128)(2,1)}, u32[]{:S(2)}) copy-start(bf16[2,256,2048]{2,1,0:T(8,128)(2,1)} %img_hbm.1) | copy-start | bytes 6291460
  1.6 0.7 %copy-start.1 = (s32[2,2,4,32]{3,2,1,0:T(4,128)S(1)}, s32[2,2,4,32]{3,2,1,0:T(4,128)}, u32[]{:S(2)}) copy-start(s32[2,2,4,32]{3,2,1,0:T(4,128)} %shift_ref.1) | copy-start | bytes 6148

commit v2 on v1

--- a/solution.py
+++ b/solution.py
@@ -55,9 +55,9 @@
         lax.fori_loop(start, stop, lambda i, _: (body(i), 0)[1], 0)
 
 
-def fit_kernel(n_ty, n_tx, lam_y, lam_x, img_hbm, shift_ref, pad_hbm, col_ref, row_ref,
-               img_v, sums_v, shift_v, e0_v, msg_v, slots_v, coef_v, zero_r, zero_c,
-               img_sem, own_sem, zero_sem, e0_send, e0_recv, msg_send, msg_recv,
+def fit_kernel(n_ty, n_tx, lam_y, lam_x, img_hbm, shift_hbm, pad_hbm, col_ref, row_ref,
+               img_v, shift_ref, sums_v, shift_v, e0_v, msg_v, slots_v, coef_v, zero_r, zero_c,
+               img_sem, shift_sem, own_sem, zero_sem, e0_send, e0_recv, msg_send, msg_recv,
                halo_send, halo_recv):
     chans, rows, cols = img_v.shape
     prow, pcol = rows // PATCH, cols // PATCH
@@ -77,6 +77,8 @@
         _, where = peer_id(p)
         pl.semaphore_signal(barrier, inc=1, device_id=where, device_id_type=MESH)
 
+    shift_load = pltpu.make_async_copy(shift_hbm, shift_ref, shift_sem)
+    shift_load.start()
     loads = []
     for c in range(chans):
         for i in range(prow):
@@ -107,6 +109,7 @@
     col_pos = (lane % pcol * PATCH).astype(jnp.float32) / SPAN_X + (PATCH / 2.0 / SPAN_X + 1.0)
     row_index = lane // per_dev * prow + lane % prow
     row_pos = (row_index * PATCH).astype(jnp.float32) / SPAN_Y + (PATCH / 2.0 / SPAN_Y + 1.0)
+    shift_load.wait()
     for q in range(2):
         for c in range(chans):
             part = shift_ref[c, q].astype(jnp.float32)
@@ -315,41 +318,62 @@
 
 BLOCK = 256
 HALF = 128
-
-
-def warp_kernel(pad_ref, col_ref, row_ref, out_ref, rows_v, rtaps_v, ctaps_v):
-    c, b = pl.program_id(0), pl.program_id(1)
-    rows = out_ref.shape[1]
+PAD = 64
+
+
+def taps(target, depth, shift):
+    low = jnp.floor(target)
+    frac = target - low
+    weights = [cubic_kernel(float(e) - frac).astype(jnp.bfloat16) for e in (-1, 0, 1, 2)]
+    shape = (depth, target.shape[1])
+    source = (lax.broadcasted_iota(jnp.int32, shape, 0) - shift).astype(jnp.float32).astype(jnp.bfloat16)
+    offset = source - (low - shift).astype(jnp.bfloat16)
+    out = jnp.zeros(shape, jnp.bfloat16)
+    for e, weight in zip((-1, 0, 1, 2), weights):
+        out = jnp.where(offset == e, jnp.broadcast_to(weight, shape), out)
+    return out
+
+
+def warp_kernel(pad_ref, col_ref, row_ref, out_hbm, rows_v, rtaps_v, ctaps_v, out_v, out_sem):
+    chans, rows, cols = out_v.shape
     depth = pad_ref.shape[1]
-
-    @pl.when((c == 0) & (b == 0))
-    def _():
-        ctaps_v[...] = jnp.zeros_like(ctaps_v)
-
-    @pl.when(b == 0)
-    def _():
-        rows_v[...] = jnp.zeros_like(rows_v)
-        disp = jnp.where(c == 0, row_ref[2:3, :], row_ref[3:4, :])
-        target = lax.broadcasted_iota(jnp.int32, (1, rows), 1).astype(jnp.float32) + HY + disp
+    steps = cols // BLOCK
+    lane_f = lax.broadcasted_iota(jnp.int32, (1, HALF), 1).astype(jnp.float32)
+    row_f = lax.broadcasted_iota(jnp.int32, (1, rows), 1).astype(jnp.float32)
+    for slot in range(2):
+        ctaps_v[slot] = jnp.zeros(ctaps_v.shape[1:], jnp.bfloat16)
+    for c in range(chans):
+        target = row_f + HY + row_ref[chans + c : chans + c + 1, :]
         source = lax.broadcasted_iota(jnp.int32, (depth, rows), 0).astype(jnp.float32)
-        rtaps_v[...] = cubic_kernel(source - target).T.astype(jnp.bfloat16)
-
-    rows_v[:, 0:BLOCK] = rows_v[:, BLOCK : 2 * BLOCK]
-    rows_v[:, BLOCK : 2 * BLOCK] = jnp.dot(
-        rtaps_v[...], pad_ref[0], preferred_element_type=jnp.float32
-    ).astype(jnp.bfloat16)
-    first = jnp.maximum(b - 1, 0) * BLOCK
-    source = lax.broadcasted_iota(jnp.int32, (2 * HALF, HALF), 0).astype(jnp.float32)
-    for h in range(BLOCK // HALF):
-        at = pl.ds(pl.multiple_of(first + h * HALF, HALF), HALF)
-        disp = jnp.where(c == 0, col_ref[0:1, at], col_ref[1:2, at])
-        target = lax.broadcasted_iota(jnp.int32, (1, HALF), 1).astype(jnp.float32) + 64.0 + disp
-        ctaps_v[64 + h * HALF : 64 + h * HALF + 2 * HALF, h * HALF : (h + 1) * HALF] = cubic_kernel(
-            source - target
-        ).astype(jnp.bfloat16)
-    out_ref[0] = jnp.dot(
-        rows_v[...], ctaps_v[...], preferred_element_type=jnp.float32
-    ).astype(jnp.bfloat16)
+        rtaps_v[c] = cubic_kernel(source - target).T.astype(jnp.bfloat16)
+    copies = []
+    for c in range(chans):
+        def row_tile(b):
+            rows_v[c, :, b * BLOCK : (b + 1) * BLOCK] = jnp.dot(
+                rtaps_v[c], pad_ref[c, :, b * BLOCK : (b + 1) * BLOCK],
+                preferred_element_type=jnp.float32,
+            ).astype(jnp.bfloat16)
+
+        row_tile(0)
+        for b in range(steps):
+            row_tile(b + 1)
+            slot = b % 2
+            for h in range(BLOCK // HALF):
+                at = b * BLOCK + h * HALF
+                target = lane_f + float(PAD) + col_ref[c : c + 1, at : at + HALF]
+                ctaps_v[slot, PAD + h * HALF : PAD + (h + 2) * HALF, h * HALF : (h + 1) * HALF] = (
+                    taps(target, 2 * HALF, HALF)
+                )
+            out_v[c, :, b * BLOCK : (b + 1) * BLOCK] = jnp.dot(
+                rows_v[c, :, b * BLOCK : (b + 2) * BLOCK], ctaps_v[slot],
+                preferred_element_type=jnp.float32,
+            ).astype(jnp.bfloat16)
+            part = (c, slice(None), pl.ds(b * BLOCK, BLOCK))
+            copy = pltpu.make_async_copy(out_v.at[part], out_hbm.at[part], out_sem.at[c * steps + b])
+            copy.start()
+            copies.append(copy)
+    for copy in copies:
+        copy.wait()
 
 
 def local(image_plane, patch_shift):
@@ -363,7 +387,7 @@
     f32 = jnp.float32
     dma = pltpu.SemaphoreType.DMA
     vmem = pl.BlockSpec(memory_space=pltpu.VMEM)
-    hbm = pl.BlockSpec(memory_space=pl.ANY)
+    hbm = pl.BlockSpec(memory_space=pltpu.HBM)
     padded, col_disp, row_disp = pl.pallas_call(
         functools.partial(fit_kernel, n_ty, n_tx, lam_y, lam_x),
         out_shape=(
@@ -371,10 +395,11 @@
             jax.ShapeDtypeStruct((8, cols), f32),
             jax.ShapeDtypeStruct((8, rows), f32),
         ),
-        in_specs=[hbm, vmem],
-        out_specs=(hbm, vmem, vmem),
+        in_specs=[hbm, hbm],
+        out_specs=(pl.BlockSpec(memory_space=pltpu.VMEM), vmem, vmem),
         scratch_shapes=[
             pltpu.VMEM((chans, rows, cols), jnp.bfloat16),
+            pltpu.VMEM(patch_shift.shape, jnp.int32),
             pltpu.VMEM((LANES, LANES), f32),
             pltpu.VMEM((2, 8, LANES), f32),
             pltpu.VMEM((8, LANES), f32),
@@ -383,28 +408,25 @@
             pltpu.VMEM((keys, 8, LANES), f32),
             pltpu.VMEM((chans, HY, cols), jnp.bfloat16),
             pltpu.VMEM((chans, rows, HX), jnp.bfloat16),
-            dma((8,)), dma((chans,)), dma((8,)), dma, dma,
+            dma((8,)), dma, dma((chans,)), dma((8,)), dma, dma,
             dma((n,)), dma((n,)), dma((8,)), dma((8,)),
         ],
         compiler_params=pltpu.CompilerParams(
             collective_id=0, has_side_effects=True, vmem_limit_bytes=32 * 2**20
         ),
     )(image_plane, patch_shift)
-    steps = cols // BLOCK
+    bf16 = jnp.bfloat16
     return pl.pallas_call(
         warp_kernel,
-        grid=(chans, steps + 1),
-        out_shape=jax.ShapeDtypeStruct((chans, rows, cols), jnp.bfloat16),
-        in_specs=[
-            pl.BlockSpec((1, high, BLOCK), lambda c, b: (c, 0, b)),
-            pl.BlockSpec((8, cols), lambda c, b: (0, 0)),
-            pl.BlockSpec((8, rows), lambda c, b: (0, 0)),
-        ],
-        out_specs=pl.BlockSpec((1, rows, BLOCK), lambda c, b: (c, 0, jnp.maximum(b - 1, 0))),
+        out_shape=jax.ShapeDtypeStruct((chans, rows, cols), bf16),
+        in_specs=[vmem, vmem, vmem],
+        out_specs=hbm,
         scratch_shapes=[
-            pltpu.VMEM((rows, 2 * BLOCK), jnp.bfloat16),
-            pltpu.VMEM((rows, high), jnp.bfloat16),
-            pltpu.VMEM((2 * BLOCK, BLOCK), jnp.bfloat16),
+            pltpu.VMEM((chans, rows, wide), bf16),
+            pltpu.VMEM((chans, rows, high), bf16),
+            pltpu.VMEM((2, 2 * BLOCK, BLOCK), bf16),
+            pltpu.VMEM((chans, rows, cols), bf16),
+            dma((chans * cols // BLOCK,)),
         ],
         compiler_params=pltpu.CompilerParams(vmem_limit_bytes=32 * 2**20),
     )(padded, col_disp, row_disp)

time: 29.1 us -> 22.2 us (0.76)
  Pallas kernels: 26.6 us -> 19.7 us
    pallas_call x1, Pallas kernels: 10.8 us -> 3.83 us  [local(): pl.pallas_call(warp_kernel, out_shape=jax.ShapeDtypeStruct((chans, rows,...]
where the time goes in v2:
time: 22.2 us; the launch traced here: 22 us
  Pallas kernels  19.7 us (89%)
  local copies, waits for them, and re-layouts  2.29 us (10%)
    pallas_call x1, Pallas kernels, local(): pl.pallas_call(functools.partial(fit_kernel, n_ty, n_tx, lam_y, lam_x), o...  15.8 us
    pallas_call x1, Pallas kernels, local(): pl.pallas_call(warp_kernel, out_shape=jax.ShapeDtypeStruct((chans, rows,...  3.83 us
    unnamed x4, local copies, waits for them, and re-layouts  2.29 us

profile of v2, /device:TPU:0, one launch (start us, length us, event | category | flops | bytes accessed | tf_op | source)
XLA Modules:
  0.0 22.0 jit_solution(10585525145069134980)
XLA Ops:
  0.0 0.0 copy-start
  0.0 1.6 %copy-done = bf16[2,256,2048]{2,1,0:T(8,128)(2,1)S(1)} copy-done((bf16[2,256,2048]{2,1,0:T(8,128)(2,1)S(1)}, bf16[2,256,2048]{2,1,0:T(8,128)(2,1)}, u32[]{:S(2)}) %copy-start) | copy-done | bytes 2097176
  1.6 0.0 copy-start.1
  1.6 0.7 %copy-done.1 = s32[2,2,4,32]{3,2,1,0:T(4,128)S(1)} copy-done((s32[2,2,4,32]{3,2,1,0:T(4,128)S(1)}, s32[2,2,4,32]{3,2,1,0:T(4,128)}, u32[]{:S(2)}) %copy-start.1) | copy-done | bytes 2072
  2.3 15.8 %shard_map.28 = (bf16[2,288,2304]{2,1,0:T(8,128)(2,1)S(1)}, f32[8,2048]{1,0:T(8,128)S(1)}, f32[8,256]{1,0:T(8,128)S(1)}) custom-call(bf16[2,256,2048]{2,1,0:T(8,128)(2,1)S(1)} %copy-done, s32[2,2,4,32]{3,2,1,0:T(4,128)S(1)} %copy-done.1), custom_call_target="tpu_custom_call" | custom-call | tf_op jit(solution)/shard_map/pallas_call | solution.py:391
  18.1 3.8 %shard_map.29 = bf16[2,256,2048]{2,1,0:T(8,128)(2,1)} custom-call(bf16[2,288,2304]{2,1,0:T(8,128)(2,1)S(1)} %get-tuple-element.8.pad_ref, f32[8,2048]{1,0:T(8,128)S(1)} %get-tuple-element.9.col_ref, f32[8,256]{1,0:T(8,128)S(1)} %get-tuple-element.10.row_ref), custom_call_target="tpu_custom_call" | custom-call | tf_op jit(solution)/shard_map/pallas_call | solution.py:419
Async XLA Ops:
  0.0 1.6 %copy-start = (bf16[2,256,2048]{2,1,0:T(8,128)(2,1)S(1)}, bf16[2,256,2048]{2,1,0:T(8,128)(2,1)}, u32[]{:S(2)}) copy-start(bf16[2,256,2048]{2,1,0:T(8,128)(2,1)} %img_hbm.1) | copy-start | bytes 6291460
  1.6 0.7 %copy-start.1 = (s32[2,2,4,32]{3,2,1,0:T(4,128)S(1)}, s32[2,2,4,32]{3,2,1,0:T(4,128)}, u32[]{:S(2)}) copy-start(s32[2,2,4,32]{3,2,1,0:T(4,128)} %shift_hbm.1) | copy-start | bytes 6148

commit v3 on v2

--- a/solution.py
+++ b/solution.py
@@ -13,7 +13,7 @@
 MAX_Y = 12
 MAX_X = 60
 HY = 16
-HX = 128
+HX = 64
 EPS = 1e-05
 LANES = 128
 MESH = pl.DeviceIdType.MESH
@@ -55,8 +55,8 @@
         lax.fori_loop(start, stop, lambda i, _: (body(i), 0)[1], 0)
 
 
-def fit_kernel(n_ty, n_tx, lam_y, lam_x, img_hbm, shift_hbm, pad_hbm, col_ref, row_ref,
-               img_v, shift_ref, sums_v, shift_v, e0_v, msg_v, slots_v, coef_v, zero_r, zero_c,
+def fit_kernel(n_ty, n_tx, lam_y, lam_x, img_hbm, shift_hbm, main_hbm, side_hbm, col_ref, row_ref,
+               img_v, shift_ref, sums_v, shift_v, e0_v, msg_v, slots_v, coef_v, pack_v, zero_v,
                img_sem, shift_sem, own_sem, zero_sem, e0_send, e0_recv, msg_send, msg_recv,
                halo_send, halo_recv):
     chans, rows, cols = img_v.shape
@@ -90,8 +90,7 @@
             copy.start()
             loads.append(copy)
     repeat_for(1, n, greet)
-    zero_r[...] = jnp.zeros_like(zero_r)
-    zero_c[...] = jnp.zeros_like(zero_c)
+    zero_v[...] = jnp.zeros_like(zero_v)
 
     sub, lane = iota(0), iota(1)
     per_chan = 2 * prow
@@ -125,7 +124,7 @@
                 sums_v[pl.ds(t * 8 + c * prow + i, 1), :] = jnp.sum(part * part, axis=0, keepdims=True)
     owns = [
         pltpu.make_async_copy(
-            img_v.at[c], pad_hbm.at[c, pl.ds(HY, rows), pl.ds(HX, cols)], own_sem.at[c]
+            img_v.at[c], main_hbm.at[c, pl.ds(HY, rows)], own_sem.at[c]
         )
         for c in range(chans)
     ]
@@ -174,27 +173,30 @@
 
     repeat_for(1, n, lambda p: msg_copy(p, me).start())
 
+    tail, head = cols - 2 * HX, 2 * HX
+    pack_v[0] = jnp.concatenate([img_v[0, :, tail + HX :], img_v[1, :, tail + HX :]], axis=1)
+    pack_v[1] = jnp.concatenate([img_v[0, :, :HX], img_v[1, :, :HX]], axis=1)
     span_y = {1: (rows - HY, 0, HY), -1: (0, HY + rows, HY), 0: (0, HY, rows)}
-    span_x = {1: (cols - HX, 0, HX), -1: (0, HX + cols, HX), 0: (0, HX, cols)}
     sides = [(0, 1), (0, -1), (1, 0), (-1, 0), (1, 1), (1, -1), (-1, 1), (-1, -1)]
-    halos, fills = [], []
+    halos = []
     for s, (dy, dx) in enumerate(sides):
         sy, qy, ly = span_y[dy]
-        sx, qx, lx = span_x[dx]
-        dst = pad_hbm.at[:, pl.ds(qy, ly), pl.ds(qx, lx)]
+        if dx == 0:
+            src, dst = img_v.at[:, pl.ds(sy, ly)], main_hbm.at[:, pl.ds(qy, ly)]
+            zeros = zero_v.at[:, pl.ds(0, ly)]
+        else:
+            side = 0 if dx == 1 else 1
+            src, dst = pack_v.at[side, pl.ds(sy, ly)], side_hbm.at[side, pl.ds(qy, ly)]
+            zeros = zero_v.at[0, pl.ds(0, ly), pl.ds(0, head)]
         to_y, to_x = ty + dy, tx + dx
         from_y, from_x = ty - dy, tx - dx
         has_to = (to_y >= 0) & (to_y < n_ty) & (to_x >= 0) & (to_x < n_tx)
         has_from = (from_y >= 0) & (from_y < n_ty) & (from_x >= 0) & (from_x < n_tx)
         halo = pltpu.make_async_remote_copy(
-            src_ref=img_v.at[:, pl.ds(sy, ly), pl.ds(sx, lx)], dst_ref=dst,
-            send_sem=halo_send.at[s], recv_sem=halo_recv.at[s],
+            src_ref=src, dst_ref=dst, send_sem=halo_send.at[s], recv_sem=halo_recv.at[s],
             device_id={"ty": to_y, "tx": to_x}, device_id_type=MESH,
         )
-        zeros = zero_c if ly == rows else zero_r
-        fill = pltpu.make_async_copy(
-            zeros.at[:, pl.ds(0, ly), pl.ds(0, lx)], dst, zero_sem.at[s]
-        )
+        fill = pltpu.make_async_copy(zeros, dst, zero_sem.at[s])
         pl.when(has_to)(halo.start)
         pl.when(jnp.logical_not(has_from))(fill.start)
         halos.append((halo, has_to, has_from, fill))
@@ -334,26 +336,58 @@
     return out
 
 
-def warp_kernel(pad_ref, col_ref, row_ref, out_hbm, rows_v, rtaps_v, ctaps_v, out_v, out_sem):
+def warp_kernel(main_hbm, side_hbm, col_hbm, row_hbm, out_hbm, pad_ref, side_v, col_ref, row_ref,
+                rows_v, rtaps_v, ctaps_v, out_v, out_sem, in_sem, small_sem):
     chans, rows, cols = out_v.shape
     depth = pad_ref.shape[1]
     steps = cols // BLOCK
+    edge = 2 * HX
+    small = [
+        pltpu.make_async_copy(row_hbm, row_ref, small_sem.at[0]),
+        pltpu.make_async_copy(side_hbm, side_v, small_sem.at[1]),
+        pltpu.make_async_copy(col_hbm, col_ref, small_sem.at[2]),
+    ]
+    loads = [
+        pltpu.make_async_copy(
+            main_hbm.at[c, :, pl.ds(b * BLOCK, BLOCK)],
+            pad_ref.at[c, :, pl.ds(edge + b * BLOCK, BLOCK)],
+            in_sem.at[c * steps + b],
+        )
+        for c in range(chans) for b in range(steps)
+    ]
+    small[0].start()
+    small[1].start()
+    loads[0].start()
+    small[2].start()
+    for load in loads[1:]:
+        load.start()
     lane_f = lax.broadcasted_iota(jnp.int32, (1, HALF), 1).astype(jnp.float32)
     row_f = lax.broadcasted_iota(jnp.int32, (1, rows), 1).astype(jnp.float32)
     for slot in range(2):
         ctaps_v[slot] = jnp.zeros(ctaps_v.shape[1:], jnp.bfloat16)
+    small[0].wait()
     for c in range(chans):
         target = row_f + HY + row_ref[chans + c : chans + c + 1, :]
         source = lax.broadcasted_iota(jnp.int32, (depth, rows), 0).astype(jnp.float32)
         rtaps_v[c] = cubic_kernel(source - target).T.astype(jnp.bfloat16)
+    small[1].wait()
+    for i in range(2):
+        whole = side_v[i]
+        other = jnp.concatenate([whole[:, HX:], whole[:, :HX]], axis=1)
+        at = 0 if i == 0 else edge + cols
+        pad_ref[i, :, at : at + edge] = other
+        pad_ref[1 - i, :, at : at + edge] = whole
     copies = []
     for c in range(chans):
         def row_tile(b):
+            if b < steps:
+                loads[c * steps + b].wait()
             rows_v[c, :, b * BLOCK : (b + 1) * BLOCK] = jnp.dot(
                 rtaps_v[c], pad_ref[c, :, b * BLOCK : (b + 1) * BLOCK],
                 preferred_element_type=jnp.float32,
             ).astype(jnp.bfloat16)
 
+        small[2].wait() if c == 0 else None
         row_tile(0)
         for b in range(steps):
             row_tile(b + 1)
@@ -383,20 +417,21 @@
     lam_y = SPAN_Y / PATCH * (cols * n_tx / PATCH) * (2.0 * rows / SPAN_Y) ** 4
     lam_x = SPAN_X / PATCH * (rows * n_ty / PATCH) * (1.0 * cols / SPAN_X) ** 4
     keys = max(n_ty * rows // SPAN_Y, n_tx * cols // SPAN_X) + 3
-    high, wide = rows + 2 * HY, cols + 2 * HX
+    high, wide = rows + 2 * HY, cols + 4 * HX
     f32 = jnp.float32
     dma = pltpu.SemaphoreType.DMA
     vmem = pl.BlockSpec(memory_space=pltpu.VMEM)
     hbm = pl.BlockSpec(memory_space=pltpu.HBM)
-    padded, col_disp, row_disp = pl.pallas_call(
+    main, side, col_disp, row_disp = pl.pallas_call(
         functools.partial(fit_kernel, n_ty, n_tx, lam_y, lam_x),
         out_shape=(
-            jax.ShapeDtypeStruct((chans, high, wide), jnp.bfloat16),
+            jax.ShapeDtypeStruct((chans, high, cols), jnp.bfloat16),
+            jax.ShapeDtypeStruct((2, high, 2 * HX), jnp.bfloat16),
             jax.ShapeDtypeStruct((8, cols), f32),
             jax.ShapeDtypeStruct((8, rows), f32),
         ),
         in_specs=[hbm, hbm],
-        out_specs=(pl.BlockSpec(memory_space=pltpu.VMEM), vmem, vmem),
+        out_specs=(hbm, hbm, vmem, vmem),
         scratch_shapes=[
             pltpu.VMEM((chans, rows, cols), jnp.bfloat16),
             pltpu.VMEM(patch_shift.shape, jnp.int32),
@@ -406,30 +441,34 @@
             pltpu.VMEM((8, LANES), f32),
             pltpu.VMEM((n, 8, LANES), f32),
             pltpu.VMEM((keys, 8, LANES), f32),
-            pltpu.VMEM((chans, HY, cols), jnp.bfloat16),
-            pltpu.VMEM((chans, rows, HX), jnp.bfloat16),
+            pltpu.VMEM((2, rows, 2 * HX), jnp.bfloat16),
+            pltpu.VMEM((chans, rows, cols), jnp.bfloat16),
             dma((8,)), dma, dma((chans,)), dma((8,)), dma, dma,
             dma((n,)), dma((n,)), dma((8,)), dma((8,)),
         ],
         compiler_params=pltpu.CompilerParams(
-            collective_id=0, has_side_effects=True, vmem_limit_bytes=32 * 2**20
+            collective_id=0, has_side_effects=True, vmem_limit_bytes=58 * 2**20
         ),
     )(image_plane, patch_shift)
     bf16 = jnp.bfloat16
     return pl.pallas_call(
         warp_kernel,
         out_shape=jax.ShapeDtypeStruct((chans, rows, cols), bf16),
-        in_specs=[vmem, vmem, vmem],
+        in_specs=[hbm, hbm, hbm, hbm],
         out_specs=hbm,
         scratch_shapes=[
+            pltpu.VMEM((chans, high, wide), bf16),
+            pltpu.VMEM((2, high, 2 * HX), bf16),
+            pltpu.VMEM((8, cols), f32),
+            pltpu.VMEM((8, rows), f32),
             pltpu.VMEM((chans, rows, wide), bf16),
             pltpu.VMEM((chans, rows, high), bf16),
             pltpu.VMEM((2, 2 * BLOCK, BLOCK), bf16),
             pltpu.VMEM((chans, rows, cols), bf16),
-            dma((chans * cols // BLOCK,)),
+            dma((chans * cols // BLOCK,)), dma((chans * cols // BLOCK,)), dma((3,)),
         ],
-        compiler_params=pltpu.CompilerParams(vmem_limit_bytes=32 * 2**20),
-    )(padded, col_disp, row_disp)
+        compiler_params=pltpu.CompilerParams(vmem_limit_bytes=58 * 2**20),
+    )(main, side, col_disp, row_disp)
 
 
 def solution(mesh):

time: 22.2 us -> 23.4 us (1.054)
  Pallas kernels: 19.7 us -> 23.2 us
  local copies, waits for them, and re-layouts: 2.29 us -> 0 us
    pallas_call x1, Pallas kernels: 3.83 us -> 9.6 us  [local(): pl.pallas_call(warp_kernel, out_shape=jax.ShapeDtypeStruct((chans, rows,...]
    unnamed x4 -> x0, local copies, waits for them, and re-layouts: 2.29 us -> none
    pallas_call x1, Pallas kernels: 15.8 us -> 13.6 us  [local(): pl.pallas_call(functools.partial(fit_kernel, n_ty, n_tx, lam_y, lam_x), o...]
where the time goes in v3:
time: 23.4 us; the launch traced here: 23.2 us
  Pallas kernels  23.2 us (99%)
    pallas_call x1, Pallas kernels, local(): pl.pallas_call(functools.partial(fit_kernel, n_ty, n_tx, lam_y, lam_x), o...  13.6 us
    pallas_call x1, Pallas kernels, local(): pl.pallas_call(warp_kernel, out_shape=jax.ShapeDtypeStruct((chans, rows,...  9.6 us

profile of v3, /device:TPU:0, one launch (start us, length us, event | category | flops | bytes accessed | tf_op | source)
XLA Modules:
  0.0 23.2 jit_solution(3959877005505676421)
XLA Ops:
  0.0 13.6 %shard_map.28 = (bf16[2,288,2048]{2,1,0:T(8,128)(2,1)}, bf16[2,288,128]{2,1,0:T(8,128)(2,1)}, f32[8,2048]{1,0:T(8,128)}, f32[8,256]{1,0:T(8,128)}) custom-call(bf16[2,256,2048]{2,1,0:T(8,128)(2,1)} %img_hbm.1, s32[2,2,4,32]{3,2,1,0:T(4,128)} %shift_hbm.1), custom_call_target="tpu_custom_call" | custom-call | tf_op jit(solution)/shard_map/pallas_call | solution.py:425
  13.6 9.6 %shard_map.29 = bf16[2,256,2048]{2,1,0:T(8,128)(2,1)} custom-call(bf16[2,288,2048]{2,1,0:T(8,128)(2,1)} %get-tuple-element.9.main_hbm, bf16[2,288,128]{2,1,0:T(8,128)(2,1)} %get-tuple-element.10.side_hbm, f32[8,2048]{1,0:T(8,128)} %get-tuple-element.11.col_hbm, f32[8,256]{1,0:T(8,128)} %get-tuple-element.12.row_hbm), custom_call_target="tpu_custom_call" | custom-call | tf_op jit(solution)/shard_map/pallas_call | solution.py:454

commit v4 on v2

--- a/solution.py
+++ b/solution.py
@@ -13,7 +13,7 @@
 MAX_Y = 12
 MAX_X = 60
 HY = 16
-HX = 128
+HX = 64
 EPS = 1e-05
 LANES = 128
 MESH = pl.DeviceIdType.MESH
@@ -55,9 +55,9 @@
         lax.fori_loop(start, stop, lambda i, _: (body(i), 0)[1], 0)
 
 
-def fit_kernel(n_ty, n_tx, lam_y, lam_x, img_hbm, shift_hbm, pad_hbm, col_ref, row_ref,
-               img_v, shift_ref, sums_v, shift_v, e0_v, msg_v, slots_v, coef_v, zero_r, zero_c,
-               img_sem, shift_sem, own_sem, zero_sem, e0_send, e0_recv, msg_send, msg_recv,
+def fit_kernel(n_ty, n_tx, lam_y, lam_x, img_v, shift_ref, pad_ref, col_ref, row_ref,
+               side_v, sums_v, shift_v, e0_v, msg_v, slots_v, coef_v, pack_v, zero_v,
+               own_sem, zero_sem, e0_send, e0_recv, msg_send, msg_recv,
                halo_send, halo_recv):
     chans, rows, cols = img_v.shape
     prow, pcol = rows // PATCH, cols // PATCH
@@ -77,21 +77,8 @@
         _, where = peer_id(p)
         pl.semaphore_signal(barrier, inc=1, device_id=where, device_id_type=MESH)
 
-    shift_load = pltpu.make_async_copy(shift_hbm, shift_ref, shift_sem)
-    shift_load.start()
-    loads = []
-    for c in range(chans):
-        for i in range(prow):
-            copy = pltpu.make_async_copy(
-                img_hbm.at[c, pl.ds(i * PATCH, PATCH)],
-                img_v.at[c, pl.ds(i * PATCH, PATCH)],
-                img_sem.at[c * prow + i],
-            )
-            copy.start()
-            loads.append(copy)
     repeat_for(1, n, greet)
-    zero_r[...] = jnp.zeros_like(zero_r)
-    zero_c[...] = jnp.zeros_like(zero_c)
+    zero_v[...] = jnp.zeros_like(zero_v)
 
     sub, lane = iota(0), iota(1)
     per_chan = 2 * prow
@@ -109,7 +96,6 @@
     col_pos = (lane % pcol * PATCH).astype(jnp.float32) / SPAN_X + (PATCH / 2.0 / SPAN_X + 1.0)
     row_index = lane // per_dev * prow + lane % prow
     row_pos = (row_index * PATCH).astype(jnp.float32) / SPAN_Y + (PATCH / 2.0 / SPAN_Y + 1.0)
-    shift_load.wait()
     for q in range(2):
         for c in range(chans):
             part = shift_ref[c, q].astype(jnp.float32)
@@ -119,13 +105,12 @@
 
     for c in range(chans):
         for i in range(prow):
-            loads[c * prow + i].wait()
             for t in range(cols // LANES):
                 part = img_v[c, pl.ds(i * PATCH, PATCH), pl.ds(t * LANES, LANES)].astype(jnp.float32)
                 sums_v[pl.ds(t * 8 + c * prow + i, 1), :] = jnp.sum(part * part, axis=0, keepdims=True)
     owns = [
         pltpu.make_async_copy(
-            img_v.at[c], pad_hbm.at[c, pl.ds(HY, rows), pl.ds(HX, cols)], own_sem.at[c]
+            img_v.at[c], pad_ref.at[c, pl.ds(HY, rows), pl.ds(2 * HX, cols)], own_sem.at[c]
         )
         for c in range(chans)
     ]
@@ -174,27 +159,30 @@
 
     repeat_for(1, n, lambda p: msg_copy(p, me).start())
 
+    tail, head = cols - 2 * HX, 2 * HX
+    pack_v[0] = jnp.concatenate([img_v[0, :, tail + HX :], img_v[1, :, tail + HX :]], axis=1)
+    pack_v[1] = jnp.concatenate([img_v[0, :, :HX], img_v[1, :, :HX]], axis=1)
     span_y = {1: (rows - HY, 0, HY), -1: (0, HY + rows, HY), 0: (0, HY, rows)}
-    span_x = {1: (cols - HX, 0, HX), -1: (0, HX + cols, HX), 0: (0, HX, cols)}
     sides = [(0, 1), (0, -1), (1, 0), (-1, 0), (1, 1), (1, -1), (-1, 1), (-1, -1)]
-    halos, fills = [], []
+    halos = []
     for s, (dy, dx) in enumerate(sides):
         sy, qy, ly = span_y[dy]
-        sx, qx, lx = span_x[dx]
-        dst = pad_hbm.at[:, pl.ds(qy, ly), pl.ds(qx, lx)]
+        if dx == 0:
+            src, dst = img_v.at[:, pl.ds(sy, ly)], pad_ref.at[:, pl.ds(qy, ly), pl.ds(2 * HX, cols)]
+            zeros = zero_v.at[:, pl.ds(0, ly)]
+        else:
+            side = 0 if dx == 1 else 1
+            src, dst = pack_v.at[side, pl.ds(sy, ly)], side_v.at[side, pl.ds(qy, ly)]
+            zeros = zero_v.at[0, pl.ds(0, ly), pl.ds(0, head)]
         to_y, to_x = ty + dy, tx + dx
         from_y, from_x = ty - dy, tx - dx
         has_to = (to_y >= 0) & (to_y < n_ty) & (to_x >= 0) & (to_x < n_tx)
         has_from = (from_y >= 0) & (from_y < n_ty) & (from_x >= 0) & (from_x < n_tx)
         halo = pltpu.make_async_remote_copy(
-            src_ref=img_v.at[:, pl.ds(sy, ly), pl.ds(sx, lx)], dst_ref=dst,
-            send_sem=halo_send.at[s], recv_sem=halo_recv.at[s],
+            src_ref=src, dst_ref=dst, send_sem=halo_send.at[s], recv_sem=halo_recv.at[s],
             device_id={"ty": to_y, "tx": to_x}, device_id_type=MESH,
         )
-        zeros = zero_c if ly == rows else zero_r
-        fill = pltpu.make_async_copy(
-            zeros.at[:, pl.ds(0, ly), pl.ds(0, lx)], dst, zero_sem.at[s]
-        )
+        fill = pltpu.make_async_copy(zeros, dst, zero_sem.at[s])
         pl.when(has_to)(halo.start)
         pl.when(jnp.logical_not(has_from))(fill.start)
         halos.append((halo, has_to, has_from, fill))
@@ -310,6 +298,12 @@
         pl.when(has_from)(halo.wait_recv)
         pl.when(jnp.logical_not(has_from))(fill.wait)
         pl.when(has_to)(halo.wait_send)
+    for i in range(2):
+        whole = side_v[i]
+        other = jnp.concatenate([whole[:, HX:], whole[:, :HX]], axis=1)
+        at = 0 if i == 0 else head + cols
+        pad_ref[i, :, at : at + head] = other
+        pad_ref[1 - i, :, at : at + head] = whole
     for own in owns:
         own.wait()
     pl.when(ch == 0)(e0_copy.wait_send)
@@ -383,7 +377,7 @@
     lam_y = SPAN_Y / PATCH * (cols * n_tx / PATCH) * (2.0 * rows / SPAN_Y) ** 4
     lam_x = SPAN_X / PATCH * (rows * n_ty / PATCH) * (1.0 * cols / SPAN_X) ** 4
     keys = max(n_ty * rows // SPAN_Y, n_tx * cols // SPAN_X) + 3
-    high, wide = rows + 2 * HY, cols + 2 * HX
+    high, wide = rows + 2 * HY, cols + 4 * HX
     f32 = jnp.float32
     dma = pltpu.SemaphoreType.DMA
     vmem = pl.BlockSpec(memory_space=pltpu.VMEM)
@@ -395,20 +389,19 @@
             jax.ShapeDtypeStruct((8, cols), f32),
             jax.ShapeDtypeStruct((8, rows), f32),
         ),
-        in_specs=[hbm, hbm],
-        out_specs=(pl.BlockSpec(memory_space=pltpu.VMEM), vmem, vmem),
+        in_specs=[vmem, vmem],
+        out_specs=(vmem, vmem, vmem),
         scratch_shapes=[
-            pltpu.VMEM((chans, rows, cols), jnp.bfloat16),
-            pltpu.VMEM(patch_shift.shape, jnp.int32),
+            pltpu.VMEM((2, high, 2 * HX), jnp.bfloat16),
             pltpu.VMEM((LANES, LANES), f32),
             pltpu.VMEM((2, 8, LANES), f32),
             pltpu.VMEM((8, LANES), f32),
             pltpu.VMEM((8, LANES), f32),
             pltpu.VMEM((n, 8, LANES), f32),
             pltpu.VMEM((keys, 8, LANES), f32),
-            pltpu.VMEM((chans, HY, cols), jnp.bfloat16),
-            pltpu.VMEM((chans, rows, HX), jnp.bfloat16),
-            dma((8,)), dma, dma((chans,)), dma((8,)), dma, dma,
+            pltpu.VMEM((2, rows, 2 * HX), jnp.bfloat16),
+            pltpu.VMEM((chans, rows, cols), jnp.bfloat16),
+            dma((chans,)), dma((8,)), dma, dma,
             dma((n,)), dma((n,)), dma((8,)), dma((8,)),
         ],
         compiler_params=pltpu.CompilerParams(

time: 22.2 us -> 19.1 us (0.86)
  Pallas kernels: 19.7 us -> 16.6 us
    pallas_call x1, Pallas kernels: 15.8 us -> 12.8 us  [local(): pl.pallas_call(functools.partial(fit_kernel, n_ty, n_tx, lam_y, lam_x), o...]
where the time goes in v4:
time: 19.1 us; the launch traced here: 18.9 us
  Pallas kernels  16.6 us (87%)
  local copies, waits for them, and re-layouts  2.29 us (12%)
    pallas_call x1, Pallas kernels, local(): pl.pallas_call(functools.partial(fit_kernel, n_ty, n_tx, lam_y, lam_x), o...  12.8 us
    pallas_call x1, Pallas kernels, local(): pl.pallas_call(warp_kernel, out_shape=jax.ShapeDtypeStruct((chans, rows,...  3.83 us
    unnamed x4, local copies, waits for them, and re-layouts  2.29 us

profile of v4, /device:TPU:0, one launch (start us, length us, event | category | flops | bytes accessed | tf_op | source)
XLA Modules:
  0.0 18.9 jit_solution(13202483267514996758)
XLA Ops:
  0.0 0.0 copy-start
  0.0 1.6 %copy-done = bf16[2,256,2048]{2,1,0:T(8,128)(2,1)S(1)} copy-done((bf16[2,256,2048]{2,1,0:T(8,128)(2,1)S(1)}, bf16[2,256,2048]{2,1,0:T(8,128)(2,1)}, u32[]{:S(2)}) %copy-start) | copy-done | bytes 2097176
  1.6 0.0 copy-start.1
  1.6 0.7 %copy-done.1 = s32[2,2,4,32]{3,2,1,0:T(4,128)S(1)} copy-done((s32[2,2,4,32]{3,2,1,0:T(4,128)S(1)}, s32[2,2,4,32]{3,2,1,0:T(4,128)}, u32[]{:S(2)}) %copy-start.1) | copy-done | bytes 2072
  2.3 12.8 %shard_map.28 = (bf16[2,288,2304]{2,1,0:T(8,128)(2,1)S(1)}, f32[8,2048]{1,0:T(8,128)S(1)}, f32[8,256]{1,0:T(8,128)S(1)}) custom-call(bf16[2,256,2048]{2,1,0:T(8,128)(2,1)S(1)} %copy-done, s32[2,2,4,32]{3,2,1,0:T(4,128)S(1)} %copy-done.1), custom_call_target="tpu_custom_call" | custom-call | tf_op jit(solution)/shard_map/pallas_call | solution.py:385
  15.1 3.8 %shard_map.29 = bf16[2,256,2048]{2,1,0:T(8,128)(2,1)} custom-call(bf16[2,288,2304]{2,1,0:T(8,128)(2,1)S(1)} %get-tuple-element.8.pad_ref, f32[8,2048]{1,0:T(8,128)S(1)} %get-tuple-element.9.col_ref, f32[8,256]{1,0:T(8,128)S(1)} %get-tuple-element.10.row_ref), custom_call_target="tpu_custom_call" | custom-call | tf_op jit(solution)/shard_map/pallas_call | solution.py:412
Async XLA Ops:
  0.0 1.6 %copy-start = (bf16[2,256,2048]{2,1,0:T(8,128)(2,1)S(1)}, bf16[2,256,2048]{2,1,0:T(8,128)(2,1)}, u32[]{:S(2)}) copy-start(bf16[2,256,2048]{2,1,0:T(8,128)(2,1)} %img_v.1) | copy-start | bytes 6291460
  1.6 0.7 %copy-start.1 = (s32[2,2,4,32]{3,2,1,0:T(4,128)S(1)}, s32[2,2,4,32]{3,2,1,0:T(4,128)}, u32[]{:S(2)}) copy-start(s32[2,2,4,32]{3,2,1,0:T(4,128)} %shift_ref.1) | copy-start | bytes 6148

commit v5 on v4

--- a/solution.py
+++ b/solution.py
@@ -80,85 +80,14 @@
     repeat_for(1, n, greet)
     zero_v[...] = jnp.zeros_like(zero_v)
 
-    sub, lane = iota(0), iota(1)
-    per_chan = 2 * prow
-    per_dev = chans * per_chan
-    ty_block = LANES // per_dev
-    blocks = (n_ty + ty_block - 1) // ty_block
-    col_sys = sub < chans
-    row_sys = (sub >= chans) & (sub < 2 * chans)
-    is_rhs = jnp.where(col_sys, (lane // pcol) % 2, (lane // prow) % 2) == 1
-    key_y = n_ty * rows // SPAN_Y + 3
-    key_x = n_tx * cols // SPAN_X + 3
-    per_y, per_x = rows * ty_block // SPAN_Y, cols // SPAN_X
-    keys = max(key_y, key_x)
-    chunks = max(n_tx, blocks)
-    col_pos = (lane % pcol * PATCH).astype(jnp.float32) / SPAN_X + (PATCH / 2.0 / SPAN_X + 1.0)
-    row_index = lane // per_dev * prow + lane % prow
-    row_pos = (row_index * PATCH).astype(jnp.float32) / SPAN_Y + (PATCH / 2.0 / SPAN_Y + 1.0)
-    for q in range(2):
-        for c in range(chans):
-            part = shift_ref[c, q].astype(jnp.float32)
-            for g in range(LANES // pcol):
-                shift_v[q, pl.ds(c * prow, prow), pl.ds(g * pcol, pcol)] = part
-    ind = (iota(0, (LANES, LANES)) // PATCH == iota(1, (LANES, LANES)) % 2).astype(jnp.float32)
-
-    for c in range(chans):
-        for i in range(prow):
-            for t in range(cols // LANES):
-                part = img_v[c, pl.ds(i * PATCH, PATCH), pl.ds(t * LANES, LANES)].astype(jnp.float32)
-                sums_v[pl.ds(t * 8 + c * prow + i, 1), :] = jnp.sum(part * part, axis=0, keepdims=True)
     owns = [
         pltpu.make_async_copy(
             img_v.at[c], pad_ref.at[c, pl.ds(HY, rows), pl.ds(2 * HX, cols)], own_sem.at[c]
         )
         for c in range(chans)
     ]
-    halves = jnp.dot(sums_v[...], ind, precision=lax.Precision.HIGHEST,
-                     preferred_element_type=jnp.float32)
-    energy = jnp.zeros((8, LANES), jnp.float32)
-    for t in range(cols // LANES):
-        energy = jnp.where(lane % pcol // 2 == t, halves[t * 8 : t * 8 + 8], energy)
-    energy = energy / (PATCH * PATCH) + EPS
-
-    pl.semaphore_wait(barrier, n)
-    e0_copy = pltpu.make_async_remote_copy(
-        src_ref=e0_v, dst_ref=e0_v, send_sem=e0_send, recv_sem=e0_recv,
-        device_id=partner, device_id_type=MESH,
-    )
-
-    @pl.when(ch == 0)
-    def _():
-        e0_v[...] = energy
-        e0_copy.start()
-
-    @pl.when(ch == 1)
-    def _():
-        e0_copy.wait_recv()
-
-    ref_energy = jnp.concatenate([e0_v[0:prow]] * chans, axis=0)
-    weight = jnp.sqrt(ref_energy * energy)
-    mine = sub // prow == lane // (2 * pcol)
-    scaled = jnp.where((lane // pcol) % 2 == 1, weight * shift_v[1], weight)
-    msg_v[0:1, :] = jnp.sum(jnp.where(mine, scaled, 0.0), axis=0, keepdims=True)
-    first = lane < pcol
-    w_rows = jnp.sum(jnp.where(first, weight, 0.0), axis=1, keepdims=True)
-    ws_rows = jnp.sum(jnp.where(first, weight * shift_v[0], 0.0), axis=1, keepdims=True)
-    base = lax.rem(ty, ty_block) * per_dev + sub // prow * per_chan + sub % prow
-    spread = jnp.where(lane == base, w_rows, jnp.where(lane == base + prow, ws_rows, 0.0))
-    msg_v[1:2, :] = jnp.sum(spread, axis=0, keepdims=True)
-    slots_v[me, 0:2] = msg_v[0:2]
-
-    def msg_copy(p, slot):
-        _, where = peer_id(p)
-        return pltpu.make_async_remote_copy(
-            src_ref=msg_v.at[pl.ds(0, 2)], dst_ref=slots_v.at[slot, pl.ds(0, 2)],
-            send_sem=msg_send.at[p], recv_sem=msg_recv.at[slot],
-            device_id=where, device_id_type=MESH,
-        )
-
-    repeat_for(1, n, lambda p: msg_copy(p, me).start())
-
+    for own in owns:
+        own.start()
     tail, head = cols - 2 * HX, 2 * HX
     pack_v[0] = jnp.concatenate([img_v[0, :, tail + HX :], img_v[1, :, tail + HX :]], axis=1)
     pack_v[1] = jnp.concatenate([img_v[0, :, :HX], img_v[1, :, :HX]], axis=1)
@@ -183,11 +112,84 @@
             device_id={"ty": to_y, "tx": to_x}, device_id_type=MESH,
         )
         fill = pltpu.make_async_copy(zeros, dst, zero_sem.at[s])
-        pl.when(has_to)(halo.start)
         pl.when(jnp.logical_not(has_from))(fill.start)
         halos.append((halo, has_to, has_from, fill))
-    for own in owns:
-        own.start()
+
+    sub, lane = iota(0), iota(1)
+    per_chan = 2 * prow
+    per_dev = chans * per_chan
+    ty_block = LANES // per_dev
+    blocks = (n_ty + ty_block - 1) // ty_block
+    col_sys = sub < chans
+    row_sys = (sub >= chans) & (sub < 2 * chans)
+    is_rhs = jnp.where(col_sys, (lane // pcol) % 2, (lane // prow) % 2) == 1
+    key_y = n_ty * rows // SPAN_Y + 3
+    key_x = n_tx * cols // SPAN_X + 3
+    per_y, per_x = rows * ty_block // SPAN_Y, cols // SPAN_X
+    keys = max(key_y, key_x)
+    chunks = max(n_tx, blocks)
+    col_pos = (lane % pcol * PATCH).astype(jnp.float32) / SPAN_X + (PATCH / 2.0 / SPAN_X + 1.0)
+    row_index = lane // per_dev * prow + lane % prow
+    row_pos = (row_index * PATCH).astype(jnp.float32) / SPAN_Y + (PATCH / 2.0 / SPAN_Y + 1.0)
+    for q in range(2):
+        for c in range(chans):
+            part = shift_ref[c, q].astype(jnp.float32)
+            for g in range(LANES // pcol):
+                shift_v[q, pl.ds(c * prow, prow), pl.ds(g * pcol, pcol)] = part
+    ind = (iota(0, (LANES, LANES)) // PATCH == iota(1, (LANES, LANES)) % 2).astype(jnp.float32)
+
+    for c in range(chans):
+        for i in range(prow):
+            for t in range(cols // LANES):
+                part = img_v[c, pl.ds(i * PATCH, PATCH), pl.ds(t * LANES, LANES)].astype(jnp.float32)
+                sums_v[pl.ds(t * 8 + c * prow + i, 1), :] = jnp.sum(part * part, axis=0, keepdims=True)
+    halves = jnp.dot(sums_v[...], ind, precision=lax.Precision.HIGHEST,
+                     preferred_element_type=jnp.float32)
+    energy = jnp.zeros((8, LANES), jnp.float32)
+    for t in range(cols // LANES):
+        energy = jnp.where(lane % pcol // 2 == t, halves[t * 8 : t * 8 + 8], energy)
+    energy = energy / (PATCH * PATCH) + EPS
+
+    pl.semaphore_wait(barrier, n)
+    e0_copy = pltpu.make_async_remote_copy(
+        src_ref=e0_v, dst_ref=e0_v, send_sem=e0_send, recv_sem=e0_recv,
+        device_id=partner, device_id_type=MESH,
+    )
+
+    @pl.when(ch == 0)
+    def _():
+        e0_v[...] = energy
+        e0_copy.start()
+
+    for halo, has_to, _, _ in halos:
+        pl.when(has_to)(halo.start)
+
+    @pl.when(ch == 1)
+    def _():
+        e0_copy.wait_recv()
+
+    ref_energy = jnp.concatenate([e0_v[0:prow]] * chans, axis=0)
+    weight = jnp.sqrt(ref_energy * energy)
+    mine = sub // prow == lane // (2 * pcol)
+    scaled = jnp.where((lane // pcol) % 2 == 1, weight * shift_v[1], weight)
+    msg_v[0:1, :] = jnp.sum(jnp.where(mine, scaled, 0.0), axis=0, keepdims=True)
+    first = lane < pcol
+    w_rows = jnp.sum(jnp.where(first, weight, 0.0), axis=1, keepdims=True)
+    ws_rows = jnp.sum(jnp.where(first, weight * shift_v[0], 0.0), axis=1, keepdims=True)
+    base = lax.rem(ty, ty_block) * per_dev + sub // prow * per_chan + sub % prow
+    spread = jnp.where(lane == base, w_rows, jnp.where(lane == base + prow, ws_rows, 0.0))
+    msg_v[1:2, :] = jnp.sum(spread, axis=0, keepdims=True)
+    slots_v[me, 0:2] = msg_v[0:2]
+
+    def msg_copy(p, slot):
+        _, where = peer_id(p)
+        return pltpu.make_async_remote_copy(
+            src_ref=msg_v.at[pl.ds(0, 2)], dst_ref=slots_v.at[slot, pl.ds(0, 2)],
+            send_sem=msg_send.at[p], recv_sem=msg_recv.at[slot],
+            device_id=where, device_id_type=MESH,
+        )
+
+    repeat_for(1, n, lambda p: msg_copy(p, me).start())
 
     bases = {}
     for t in range(chunks):

time: 19.1 us -> 19.3 us (1.010)
  Pallas kernels: 16.6 us -> 16.8 us
where the time goes in v5:
time: 19.3 us; the launch traced here: 19.1 us
  Pallas kernels  16.8 us (87%)
  local copies, waits for them, and re-layouts  2.29 us (12%)
    pallas_call x1, Pallas kernels, local(): pl.pallas_call(functools.partial(fit_kernel, n_ty, n_tx, lam_y, lam_x), o...  13 us
    pallas_call x1, Pallas kernels, local(): pl.pallas_call(warp_kernel, out_shape=jax.ShapeDtypeStruct((chans, rows,...  3.83 us
    unnamed x4, local copies, waits for them, and re-layouts  2.29 us

profile of v5, /device:TPU:0, one launch (start us, length us, event | category | flops | bytes accessed | tf_op | source)
XLA Modules:
  0.0 19.1 jit_solution(2202341874165047470)
XLA Ops:
  0.0 0.0 copy-start
  0.0 1.6 %copy-done = bf16[2,256,2048]{2,1,0:T(8,128)(2,1)S(1)} copy-done((bf16[2,256,2048]{2,1,0:T(8,128)(2,1)S(1)}, bf16[2,256,2048]{2,1,0:T(8,128)(2,1)}, u32[]{:S(2)}) %copy-start) | copy-done | bytes 2097176
  1.6 0.0 copy-start.1
  1.6 0.7 %copy-done.1 = s32[2,2,4,32]{3,2,1,0:T(4,128)S(1)} copy-done((s32[2,2,4,32]{3,2,1,0:T(4,128)S(1)}, s32[2,2,4,32]{3,2,1,0:T(4,128)}, u32[]{:S(2)}) %copy-start.1) | copy-done | bytes 2072
  2.3 13.0 %shard_map.28 = (bf16[2,288,2304]{2,1,0:T(8,128)(2,1)S(1)}, f32[8,2048]{1,0:T(8,128)S(1)}, f32[8,256]{1,0:T(8,128)S(1)}) custom-call(bf16[2,256,2048]{2,1,0:T(8,128)(2,1)S(1)} %copy-done, s32[2,2,4,32]{3,2,1,0:T(4,128)S(1)} %copy-done.1), custom_call_target="tpu_custom_call" | custom-call | tf_op jit(solution)/shard_map/pallas_call | solution.py:387
  15.3 3.8 %shard_map.29 = bf16[2,256,2048]{2,1,0:T(8,128)(2,1)} custom-call(bf16[2,288,2304]{2,1,0:T(8,128)(2,1)S(1)} %get-tuple-element.8.pad_ref, f32[8,2048]{1,0:T(8,128)S(1)} %get-tuple-element.9.col_ref, f32[8,256]{1,0:T(8,128)S(1)} %get-tuple-element.10.row_ref), custom_call_target="tpu_custom_call" | custom-call | tf_op jit(solution)/shard_map/pallas_call | solution.py:414
Async XLA Ops:
  0.0 1.6 %copy-start = (bf16[2,256,2048]{2,1,0:T(8,128)(2,1)S(1)}, bf16[2,256,2048]{2,1,0:T(8,128)(2,1)}, u32[]{:S(2)}) copy-start(bf16[2,256,2048]{2,1,0:T(8,128)(2,1)} %img_v.1) | copy-start | bytes 6291460
  1.6 0.7 %copy-start.1 = (s32[2,2,4,32]{3,2,1,0:T(4,128)S(1)}, s32[2,2,4,32]{3,2,1,0:T(4,128)}, u32[]{:S(2)}) copy-start(s32[2,2,4,32]{3,2,1,0:T(4,128)} %shift_ref.1) | copy-start | bytes 6148

commit v6 on v5

--- a/solution.py
+++ b/solution.py
@@ -161,9 +161,6 @@
         e0_v[...] = energy
         e0_copy.start()
 
-    for halo, has_to, _, _ in halos:
-        pl.when(has_to)(halo.start)
-
     @pl.when(ch == 1)
     def _():
         e0_copy.wait_recv()
@@ -190,6 +187,8 @@
         )
 
     repeat_for(1, n, lambda p: msg_copy(p, me).start())
+    for halo, has_to, _, _ in halos:
+        pl.when(has_to)(halo.start)
 
     bases = {}
     for t in range(chunks):

time: 19.3 us -> 19.1 us (0.990)
  Pallas kernels: 16.8 us -> 16.6 us
where the time goes in v6:
time: 19.1 us; the launch traced here: 18.9 us
  Pallas kernels  16.6 us (87%)
  local copies, waits for them, and re-layouts  2.29 us (12%)
    pallas_call x1, Pallas kernels, local(): pl.pallas_call(functools.partial(fit_kernel, n_ty, n_tx, lam_y, lam_x), o...  12.8 us
    pallas_call x1, Pallas kernels, local(): pl.pallas_call(warp_kernel, out_shape=jax.ShapeDtypeStruct((chans, rows,...  3.83 us
    unnamed x4, local copies, waits for them, and re-layouts  2.29 us

profile of v6, /device:TPU:0, one launch (start us, length us, event | category | flops | bytes accessed | tf_op | source)
XLA Modules:
  0.0 18.9 jit_solution(4971471843256055888)
XLA Ops:
  0.0 0.0 copy-start
  0.0 1.6 %copy-done = bf16[2,256,2048]{2,1,0:T(8,128)(2,1)S(1)} copy-done((bf16[2,256,2048]{2,1,0:T(8,128)(2,1)S(1)}, bf16[2,256,2048]{2,1,0:T(8,128)(2,1)}, u32[]{:S(2)}) %copy-start) | copy-done | bytes 2097176
  1.6 0.0 copy-start.1
  1.6 0.7 %copy-done.1 = s32[2,2,4,32]{3,2,1,0:T(4,128)S(1)} copy-done((s32[2,2,4,32]{3,2,1,0:T(4,128)S(1)}, s32[2,2,4,32]{3,2,1,0:T(4,128)}, u32[]{:S(2)}) %copy-start.1) | copy-done | bytes 2072
  2.3 12.8 %shard_map.28 = (bf16[2,288,2304]{2,1,0:T(8,128)(2,1)S(1)}, f32[8,2048]{1,0:T(8,128)S(1)}, f32[8,256]{1,0:T(8,128)S(1)}) custom-call(bf16[2,256,2048]{2,1,0:T(8,128)(2,1)S(1)} %copy-done, s32[2,2,4,32]{3,2,1,0:T(4,128)S(1)} %copy-done.1), custom_call_target="tpu_custom_call" | custom-call | tf_op jit(solution)/shard_map/pallas_call | solution.py:386
  15.1 3.8 %shard_map.29 = bf16[2,256,2048]{2,1,0:T(8,128)(2,1)} custom-call(bf16[2,288,2304]{2,1,0:T(8,128)(2,1)S(1)} %get-tuple-element.8.pad_ref, f32[8,2048]{1,0:T(8,128)S(1)} %get-tuple-element.9.col_ref, f32[8,256]{1,0:T(8,128)S(1)} %get-tuple-element.10.row_ref), custom_call_target="tpu_custom_call" | custom-call | tf_op jit(solution)/shard_map/pallas_call | solution.py:413
Async XLA Ops:
  0.0 1.6 %copy-start = (bf16[2,256,2048]{2,1,0:T(8,128)(2,1)S(1)}, bf16[2,256,2048]{2,1,0:T(8,128)(2,1)}, u32[]{:S(2)}) copy-start(bf16[2,256,2048]{2,1,0:T(8,128)(2,1)} %img_v.1) | copy-start | bytes 6291460
  1.6 0.7 %copy-start.1 = (s32[2,2,4,32]{3,2,1,0:T(4,128)S(1)}, s32[2,2,4,32]{3,2,1,0:T(4,128)}, u32[]{:S(2)}) copy-start(s32[2,2,4,32]{3,2,1,0:T(4,128)} %shift_ref.1) | copy-start | bytes 6148
